TPU v7x, 32 devices: a whole 2x2x4 slice. The times are simulated.
32 devices in a mesh: rows: 8 (over z, y), feat: 4 (over x, core).
Axes of the slice: x: 2, y: 2, z: 4, core: 2. Of those that a mesh axis runs over, the one named last changes fastest.
Arguments:
- features: bfloat16 [32768, 128], P('rows', 'feat'), may hold values from -8 to 8
- lengths: int32 [8, 6], P('rows'), may hold values from 102 to 3586, as said below
- train_counts: int32 [8, 6], P('rows'), may hold values from 51 to 3585, as said below
- used_features: int32 [8, 6], P('rows'), may hold values from 50 to 100
- w_enc: bfloat16 [128, 512], P('feat'), may hold values from -0.625 to 0.625
- b_enc: float32 [512], replicated, may hold values from -3 to 3
- w_qkv: bfloat16 [512, 1536], replicated, may hold values from -0.25 to 0.25
- b_query: float32 [512], replicated, may hold values from -3 to 3
- b_value: float32 [512], replicated, may hold values from -3 to 3
- w_out: bfloat16 [512, 512], replicated, may hold values from -2 to 2
- b_out: float32 [512], replicated, may hold values from -2 to 2
- gain_one: float32 [512], replicated, may hold values from 0.5 to 1.5
- shift_one: float32 [512], replicated, may hold values from -2 to 2
- w_up: bfloat16 [512, 1024], replicated, may hold values from -0.25 to 0.25
- b_up: float32 [1024], replicated, may hold values from -3 to 3
- w_down: bfloat16 [1024, 512], replicated, may hold values from -0.25 to 0.25
- b_down: float32 [512], replicated, may hold values from -2 to 2
- gain_two: float32 [512], replicated, may hold values from 0.5 to 1.5
- shift_two: float32 [512], replicated, may hold values from -2 to 2
- cotangent: bfloat16 [32768, 512], P(('rows', 'feat')), may hold values from -6 to 6
Outputs:
- output: bfloat16 [32768, 512], P(('rows', 'feat'))
- grad_features: float32 [32768, 128], P('rows', 'feat')
- grad_w_enc: float32 [128, 512], P('feat')
- grad_b_enc: float32 [512], replicated
- grad_w_qkv: float32 [512, 1536], replicated
- grad_b_query: float32 [512], replicated
- grad_b_value: float32 [512], replicated
- grad_w_out: float32 [512, 512], replicated
- grad_b_out: float32 [512], replicated
- grad_gain_one: float32 [512], replicated
- grad_shift_one: float32 [512], replicated
- grad_w_up: float32 [512, 1024], replicated
- grad_b_up: float32 [1024], replicated
- grad_w_down: float32 [1024, 512], replicated
- grad_b_down: float32 [512], replicated
- grad_gain_two: float32 [512], replicated
- grad_shift_two: float32 [512], replicated
Inputs may be any that keep to these rules, and one draw needn't show every extreme that they name: The lengths of a group sum to 4096; in each group one table, at a place drawn from the seed, holds more than half of the group's rows. `train_counts`: each table has at least lengths // 2 and fewer than all of its rows as train rows.
All inputs are finite; a program needn't handle non-finite values.
Results may differ from a plain program's by a relative error of at most 0.015.
Values may be sent and summed in bfloat16 or wider, within the bound.
A program may use at most 256 MiB of HBM per device.

v0:
```python
import math

import jax
import jax.numpy as jnp
from jax import lax
from jax.sharding import PartitionSpec as P

HEADS = 4
HD = 128
FEATS = 100


HIGH = lax.Precision.HIGHEST


def layout(table_len, train_count, group_rows):
    tokens_at = jnp.arange(group_rows, dtype=jnp.int32)
    table_end = jnp.cumsum(table_len)
    starts = table_end - table_len
    inside = (tokens_at[:, None] >= starts[None, :]) & (tokens_at[:, None] < table_end[None, :])
    member = inside.astype(jnp.float32)
    learned = inside & (tokens_at[:, None] < (starts + train_count)[None, :])
    is_train = jnp.sum(learned.astype(jnp.float32), axis=1)
    table_of = jnp.sum((tokens_at[:, None] >= table_end[None, :]).astype(jnp.int32), axis=1)
    return (member, is_train, table_of)


def normalized(values, member, is_train, train_count, used_count, feature_col):
    train_rows = train_count.astype(jnp.float32)[:, None]
    col_mean = (
        jnp.einsum("tg,tf->gf", member, values * is_train[:, None], precision=HIGH) / train_rows
    )
    centred = values - jnp.dot(member, col_mean, precision=HIGH)
    col_var = (
        jnp.einsum("tg,tf->gf", member, centred * centred * is_train[:, None], precision=HIGH)
        / train_rows
    )
    keeper = (feature_col[None, :] < used_count[:, None]).astype(jnp.float32)
    factor = (
        lax.rsqrt(jnp.maximum(col_var, 0.25))
        * jnp.sqrt(FEATS / used_count.astype(jnp.float32))[:, None]
        * keeper
    )
    return centred * jnp.dot(member, factor, precision=HIGH)


def layer_norm(values):
    centre = values - jnp.mean(values, axis=1, keepdims=True)
    rstd = lax.rsqrt(jnp.mean(centre * centre, axis=1, keepdims=True) + 1e-05)
    return (centre * rstd, rstd)


def norm_back(grad_normed, normed, rstd):
    first = jnp.mean(grad_normed, axis=1, keepdims=True)
    second = jnp.mean(grad_normed * normed, axis=1, keepdims=True)
    return rstd * (grad_normed - first - normed * second)


def gelu_exact(values):
    return jax.nn.gelu(values, approximate=False)


def per_device(
    features,
    lengths,
    train_counts,
    used_features,
    w_enc,
    b_enc,
    w_qkv,
    b_query,
    b_value,
    w_out,
    b_out,
    gain_one,
    shift_one,
    w_up,
    b_up,
    w_down,
    b_down,
    gain_two,
    shift_two,
    cotangent,
):
    feat_count = lax.axis_size("feat")
    feat_index = lax.axis_index("feat")
    group_rows = features.shape[0]
    feat_cols = features.shape[1]
    model_width = w_qkv.shape[0]
    quarter = group_rows // feat_count
    table_len = lengths[0]
    train_count = train_counts[0]
    used_count = used_features[0]
    member, is_train, table_of = layout(table_len, train_count, group_rows)
    feature_col = feat_index * feat_cols + jnp.arange(feat_cols, dtype=jnp.int32)

    def normalize(values):
        return normalized(values, member, is_train, train_count, used_count, feature_col)

    normed, norm_pull = jax.vjp(normalize, features.astype(jnp.float32))
    normed_low = normed.astype(jnp.bfloat16)
    encoded = (
        lax.psum_scatter(
            jnp.dot(normed_low, w_enc, preferred_element_type=jnp.float32),
            "feat",
            scatter_dimension=0,
            tiled=True,
        )
        + b_enc
    )
    enc_low = encoded.astype(jnp.bfloat16)
    projected = jnp.dot(enc_low, w_qkv, preferred_element_type=jnp.float32)
    query_low = (projected[:, :model_width] + b_query).astype(jnp.bfloat16)
    key_low = projected[:, model_width : 2 * model_width].astype(jnp.bfloat16)
    value_low = (projected[:, 2 * model_width :] + b_value).astype(jnp.bfloat16)
    keys_all, values_all = (
        lax.all_gather(key_low, "feat", axis=0, tiled=True),
        lax.all_gather(value_low, "feat", axis=0, tiled=True),
    )
    table_mine = lax.dynamic_slice_in_dim(table_of, feat_index * quarter, quarter)
    block_rows = min(512, quarter)
    block_count = quarter // block_rows
    inv_root = 1.0 / math.sqrt(HD)
    key_train = is_train[None, :] > 0.5

    def head_scores(query_blk, allowed, lower):
        scores = (
            jnp.einsum(
                "qd,kd->qk",
                query_blk[:, lower : lower + HD],
                keys_all[:, lower : lower + HD],
                preferred_element_type=jnp.float32,
            )
            * inv_root
        )
        return jnp.where(allowed, scores, -1e30)

    def forward_block(args):
        query_blk, table_blk = args
        allowed = (table_blk[:, None] == table_of[None, :]) & key_train
        pieces = []
        logsums = []
        for which_head in range(HEADS):
            lower = which_head * HD
            scores = head_scores(query_blk, allowed, lower)
            peak = jnp.max(scores, axis=1, keepdims=True)
            logsum = peak + jnp.log(jnp.sum(jnp.exp(scores - peak), axis=1, keepdims=True))
            probs = jnp.exp(scores - logsum)
            pieces.append(
                jnp.dot(
                    probs.astype(jnp.bfloat16),
                    values_all[:, lower : lower + HD],
                    preferred_element_type=jnp.float32,
                )
            )
            logsums.append(logsum[:, 0])
        return (jnp.concatenate(pieces, axis=1), jnp.stack(logsums, axis=1))

    query_blocks = query_low.reshape(block_count, block_rows, model_width)
    table_blocks = table_mine.reshape(block_count, block_rows)
    attended, block_logsums = lax.map(forward_block, (query_blocks, table_blocks))
    attn_low = attended.reshape(quarter, model_width).astype(jnp.bfloat16)
    branch = jnp.dot(attn_low, w_out, preferred_element_type=jnp.float32) + b_out
    normed_one, rstd_one = layer_norm(encoded + branch)
    out_one = normed_one * gain_one + shift_one
    out_one_low = out_one.astype(jnp.bfloat16)
    pre_act = jnp.dot(out_one_low, w_up, preferred_element_type=jnp.float32) + b_up
    activ, gelu_pull = jax.vjp(gelu_exact, pre_act)
    activ_low = activ.astype(jnp.bfloat16)
    ffn = jnp.dot(activ_low, w_down, preferred_element_type=jnp.float32) + b_down
    normed_two, rstd_two = layer_norm(out_one + ffn)
    output = (normed_two * gain_two + shift_two).astype(jnp.bfloat16)
    grad_out = cotangent.astype(jnp.float32)
    grad_gain_two = jnp.sum(grad_out * normed_two, axis=0)
    grad_shift_two = jnp.sum(grad_out, axis=0)
    grad_two = norm_back(grad_out * gain_two, normed_two, rstd_two)
    grad_ffn_low = grad_two.astype(jnp.bfloat16)
    grad_w_down = jnp.einsum(
        "ti,to->io", activ_low, grad_ffn_low, preferred_element_type=jnp.float32
    )
    grad_b_down = jnp.sum(grad_ffn_low.astype(jnp.float32), axis=0)
    grad_act = jnp.einsum("to,io->ti", grad_ffn_low, w_down, preferred_element_type=jnp.float32)
    grad_pre_low = gelu_pull(grad_act)[0].astype(jnp.bfloat16)
    grad_w_up = jnp.einsum(
        "ti,to->io", out_one_low, grad_pre_low, preferred_element_type=jnp.float32
    )
    grad_b_up = jnp.sum(grad_pre_low.astype(jnp.float32), axis=0)
    grad_one = (
        jnp.einsum("to,io->ti", grad_pre_low, w_up, preferred_element_type=jnp.float32) + grad_two
    )
    grad_gain_one = jnp.sum(grad_one * normed_one, axis=0)
    grad_shift_one = jnp.sum(grad_one, axis=0)
    grad_res = norm_back(grad_one * gain_one, normed_one, rstd_one)
    grad_branch_low = grad_res.astype(jnp.bfloat16)
    grad_w_out = jnp.einsum(
        "ti,to->io", attn_low, grad_branch_low, preferred_element_type=jnp.float32
    )
    grad_b_out = jnp.sum(grad_branch_low.astype(jnp.float32), axis=0)
    grad_att_low = jnp.einsum(
        "to,io->ti", grad_branch_low, w_out, preferred_element_type=jnp.float32
    ).astype(jnp.bfloat16)
    grad_blocks = grad_att_low.reshape(block_count, block_rows, model_width)

    def backward_block(carry, args):
        key_grad, value_grad = carry
        query_blk, table_blk, grad_blk, logsum_blk = args
        allowed = (table_blk[:, None] == table_of[None, :]) & key_train
        query_parts = []
        key_parts = []
        value_parts = []
        for which_head in range(HEADS):
            lower = which_head * HD
            scores = head_scores(query_blk, allowed, lower)
            probs = jnp.exp(scores - logsum_blk[:, which_head][:, None])
            grad_head = grad_blk[:, lower : lower + HD]
            dprobs = jnp.einsum(
                "qd,kd->qk",
                grad_head,
                values_all[:, lower : lower + HD],
                preferred_element_type=jnp.float32,
            )
            dprob_sum = jnp.sum(dprobs * probs, axis=1, keepdims=True)
            dscore_low = (probs * (dprobs - dprob_sum)).astype(jnp.bfloat16)
            query_parts.append(
                jnp.dot(
                    dscore_low, keys_all[:, lower : lower + HD], preferred_element_type=jnp.float32
                )
                * inv_root
            )
            key_parts.append(
                jnp.einsum(
                    "qk,qd->kd",
                    dscore_low,
                    query_blk[:, lower : lower + HD],
                    preferred_element_type=jnp.float32,
                )
                * inv_root
            )
            value_parts.append(
                jnp.einsum(
                    "qk,qd->kd",
                    probs.astype(jnp.bfloat16),
                    grad_head,
                    preferred_element_type=jnp.float32,
                )
            )
        key_grad = key_grad + jnp.concatenate(key_parts, axis=1)
        value_grad = value_grad + jnp.concatenate(value_parts, axis=1)
        return ((key_grad, value_grad), jnp.concatenate(query_parts, axis=1))

    empty = jnp.zeros((group_rows, model_width), jnp.float32)
    (key_grad, value_grad), query_grad = lax.scan(
        backward_block, (empty, empty), (query_blocks, table_blocks, grad_blocks, block_logsums)
    )
    key_grad_mine, value_grad_mine = (
        lax.psum_scatter(
            key_grad.astype(jnp.bfloat16), "feat", scatter_dimension=0, tiled=True
        ).astype(jnp.float32),
        lax.psum_scatter(
            value_grad.astype(jnp.bfloat16), "feat", scatter_dimension=0, tiled=True
        ).astype(jnp.float32),
    )
    grad_proj_low = jnp.concatenate(
        [query_grad.reshape(quarter, model_width), key_grad_mine, value_grad_mine], axis=1
    ).astype(jnp.bfloat16)
    grad_w_qkv = jnp.einsum("ti,to->io", enc_low, grad_proj_low, preferred_element_type=jnp.float32)
    grad_b_query = jnp.sum(grad_proj_low[:, :model_width].astype(jnp.float32), axis=0)
    grad_b_value = jnp.sum(grad_proj_low[:, 2 * model_width :].astype(jnp.float32), axis=0)
    grad_enc = (
        jnp.einsum("to,io->ti", grad_proj_low, w_qkv, preferred_element_type=jnp.float32) + grad_res
    )
    grad_enc_low = grad_enc.astype(jnp.bfloat16)
    grad_b_enc = jnp.sum(grad_enc_low.astype(jnp.float32), axis=0)
    grad_enc_all = lax.all_gather(grad_enc_low, "feat", axis=0, tiled=True)
    grad_w_enc_part = jnp.einsum(
        "tf,te->fe", normed_low, grad_enc_all, preferred_element_type=jnp.float32
    )
    grad_normed = jnp.einsum("te,fe->tf", grad_enc_all, w_enc, preferred_element_type=jnp.float32)
    grad_w_enc = lax.psum(grad_w_enc_part.astype(jnp.bfloat16), "rows").astype(jnp.float32)
    grad_features = norm_pull(grad_normed)[0]
    summed = lax.psum(
        (
            grad_b_enc,
            grad_w_qkv,
            grad_b_query,
            grad_b_value,
            grad_w_out,
            grad_b_out,
            grad_gain_one,
            grad_shift_one,
            grad_w_up,
            grad_b_up,
            grad_w_down,
            grad_b_down,
            grad_gain_two,
            grad_shift_two,
        ),
        ("rows", "feat"),
    )
    return (
        output,
        grad_features,
        grad_w_enc,
        summed[0],
        summed[1],
        summed[2],
        summed[3],
        summed[4],
        summed[5],
        summed[6],
        summed[7],
        summed[8],
        summed[9],
        summed[10],
        summed[11],
        summed[12],
        summed[13],
    )


def solution(mesh):
    in_specs = (
        P("rows", "feat"),
        P("rows", None),
        P("rows", None),
        P("rows", None),
        P("feat", None),
        P(),
        P(),
        P(),
        P(),
        P(),
        P(),
        P(),
        P(),
        P(),
        P(),
        P(),
        P(),
        P(),
        P(),
        P(("rows", "feat"), None),
    )
    out_specs = (
        P(("rows", "feat"), None),
        P("rows", "feat"),
        P("feat", None),
        P(),
        P(),
        P(),
        P(),
        P(),
        P(),
        P(),
        P(),
        P(),
        P(),
        P(),
        P(),
        P(),
        P(),
    )
    return jax.shard_map(
        per_device, mesh=mesh, in_specs=in_specs, out_specs=out_specs, check_vma=False
    )
```

profile of v0, /device:TPU:0, one launch (start us, length us, event | category | flops | bytes accessed | tf_op | source)
XLA Modules:
  0.0 870.4 jit_solution(1469322319419382275)
XLA Ops:
  16.1 5.3 fusion.133
  21.5 74.5 %reduce-scatter.4.cloned.1.call-done = f32[1024,512]{1,0:T(8,128)} async-done(((f32[4096,512]{1,0:T(8,128)}), f32[1024,512]{1,0:T(8,128)}) %reduce-scatter.4.cloned.1.call-update) | async-done | bytes 2097168 | tf_op jit(solution)/shard_map/reduce_scatter | solution.py:103
  108.3 30.3 %all-gather.6.cloned.1.call-done = bf16[4096,512]{1,0:T(8,128)(2,1)} async-done(((bf16[1024,512]{1,0:T(8,128)(2,1)}), bf16[4096,512]{1,0:T(8,128)(2,1)}) %all-gather.6.cloned.1.call-update) | async-done | bytes 4194320 | tf_op jit(solution)/shard_map/all_gather | solution.py:118
  138.6 36.7 %all-gather.4.cloned.1.call-done = bf16[4096,512]{1,0:T(8,128)(2,1)} async-done(((bf16[1024,512]{1,0:T(8,128)(2,1)}), bf16[4096,512]{1,0:T(8,128)(2,1)}) %all-gather.4.cloned.1.call-update) | async-done | bytes 4194320 | tf_op jit(solution)/shard_map/all_gather | solution.py:117
  176.4 57.6 %while.27 = (s32[]{:T(128)}, bf16[2,512,512]{2,1,0:T(8,128)(2,1)}, f32[2,512,4]{1,2,0:T(4,128)S(1)}, s32[2,512]{1,0:T(2,128)S(1)}, s32[4096]{0:T(1024)}, /*index...) while((s32[]{:T(128)}, bf16[2,512,512]{2,1,0:T(8,128)(2,1)}, ...), condition=%wide.region_13.14_spmd, body=%wide.region_4.13_spmd.sunk | while | flops 4372566016 | bytes 148025520 | solution.py:161
  178.0 3.6 fusion.226
  206.5 3.6 fusion.226
  237.5 9.8 %multiply_convert_fusion.4 = (bf16[1024,1024]{1,0:T(8,128)(2,1)S(1)}, f32[1024,1024]{1,0:T(8,128)S(1)}, f32[1024,1024]{1,0:T(8,128)S(1)}) fusion(f32[1024]{0:T(1024)S(1)} %copy-done.70, bf16[512,1024]{1,0:T(8,128)(2,1)S(1)} %copy-done.68, f32[1024,512]{1,0:T(8,128)S(1)} %get-tuple-element.274, f32[512]{0:T(512)S(1)} %copy-done.73, f32[512]{0:T(512)S(1)} %copy-done.62, ...), kind=kOutput, calls=%fused_computation.121 | convolution fusion | flops 1145569280 | bytes 13647872 | tf_op jit(solution)/shard_map/dot_general | solution.py:167
  265.4 262.5 %while.28 = (s32[]{:T(128)}, f32[4096,512]{0,1:T(8,128)}, f32[4096,512]{0,1:T(8,128)}, bf16[2,512,512]{2,1,0:T(8,128)(2,1)}, s32[2,512]{1,0:T(2,128)S(1)}, /*ind...) while((s32[]{:T(128)}, f32[4096,512]{0,1:T(8,128)}, ...), condition=%wide.region_27.28_spmd.clone, body=%wide.region_22.27_spmd.clone.sunk | while | flops 10855380992 | bytes 618296000 | solution.py:252
  268.1 4.3 subtract_exponential_fusion.11
  277.7 3.5 subtract_exponential_fusion.10
  285.2 3.6 subtract_exponential_fusion.9
  292.6 3.7 subtract_exponential_fusion.8
  300.2 5.8 multiply_reduce_fusion.13
  306.1 7.9 multiply_convert_fusion.10
  320.1 5.8 multiply_reduce_fusion.14
  325.9 7.9 multiply_convert_fusion.11
  336.8 3.6 convolution_multiply_fusion.19
  340.4 5.8 multiply_reduce_fusion.15
  346.2 7.9 multiply_convert_fusion.12
  360.3 5.8 multiply_reduce_fusion.16
  366.1 7.9 multiply_convert_fusion.13
  380.3 9.4 %maximum_add_fusion.3 = (f32[4096,512]{0,1:T(8,128)}, f32[4096,512]{0,1:T(8,128)}) fusion(f32[4096,128]{0,1:T(8,128)S(1)} %copy-done.10, f32[4096,128]{0,1:T(8,128)S(1)} %copy-done.11, f32[4096,128]{0,1:T(8,128)} %convolution_multiply_fusion.20, f32[4096,128]{0,1:T(8,128)} %convolution_multiply_fusion.21, f32[4096,512]{0,1:T(8,128)} %get-tuple-element.506, ...), kind=kLoop, calls=%fused_computation.43.clone.1 | loop fusion | flops 20971520 | bytes 50331648 | tf_op jit(solution)/shard_map/while/body/eval_jaxpr/add | solution.py:247
  393.2 4.3 subtract_exponential_fusion.11
  402.8 3.5 subtract_exponential_fusion.10
  410.3 3.6 subtract_exponential_fusion.9
  417.8 4.0 subtract_exponential_fusion.8
  425.6 5.8 multiply_reduce_fusion.13
  431.4 7.9 multiply_convert_fusion.10
  445.5 5.8 multiply_reduce_fusion.14
  451.3 7.9 multiply_convert_fusion.11
  465.5 5.8 multiply_reduce_fusion.15
  471.3 7.9 multiply_convert_fusion.12
  485.4 5.8 multiply_reduce_fusion.16
  491.2 7.9 multiply_convert_fusion.13
  505.4 13.7 %maximum_add_fusion.3 = (f32[4096,512]{0,1:T(8,128)}, f32[4096,512]{0,1:T(8,128)}) fusion(f32[4096,128]{0,1:T(8,128)S(1)} %copy-done.10, f32[4096,128]{0,1:T(8,128)S(1)} %copy-done.11, f32[4096,128]{0,1:T(8,128)} %convolution_multiply_fusion.20, f32[4096,128]{0,1:T(8,128)} %convolution_multiply_fusion.21, f32[4096,512]{0,1:T(8,128)} %get-tuple-element.506, ...), kind=kLoop, calls=%fused_computation.43.clone.1 | loop fusion | flops 20971520 | bytes 50331648 | tf_op jit(solution)/shard_map/while/body/eval_jaxpr/add | solution.py:247
  527.9 7.3 copy.46
  535.3 7.8 copy.47
  543.2 36.7 %reduce-scatter.6.cloned.1.call-done = bf16[1024,512]{1,0:T(8,128)(2,1)} async-done(((bf16[4096,512]{1,0:T(8,128)(2,1)}), bf16[1024,512]{1,0:T(8,128)(2,1)}) %reduce-scatter.6.cloned.1.call-update) | async-done | bytes 1048592 | tf_op jit(solution)/shard_map/reduce_scatter | solution.py:256
  579.9 46.9 %reduce-scatter.8.cloned.1.call-done = bf16[1024,512]{1,0:T(8,128)(2,1)} async-done(((bf16[4096,512]{1,0:T(8,128)(2,1)}), bf16[1024,512]{1,0:T(8,128)(2,1)}) %reduce-scatter.8.cloned.1.call-update) | async-done | bytes 1048592 | tf_op jit(solution)/shard_map/reduce_scatter | solution.py:259
  626.8 5.0 convert_reduce_fusion.6
  632.0 3.8 fusion.104
  641.5 3.6 fusion.79
  646.9 40.4 %all-reduce = (f32[512]{0:T(512)}, f32[512]{0:T(512)}, f32[512]{0:T(512)}, f32[512]{0:T(512)}, f32[512]{0:T(512)}, /*index=5*/f32[512]{0:T(512)}, f32[1024]{0:T(1024)}, f32[512]{0:T(512)}, f32[512]{0:T(512)}, f32[512]{0:T(512)}) all-reduce(f32[512]{0:T(512)S(1)} %get-tuple-element.279, ...), channel_id=1, replica_groups=mesh['rows'=8,'feat'=4] {'rows','feat'}, use_global_device_ids=true, to_apply=%region_32.33 | all-reduce | flops 5632 | bytes 45056 | tf_op jit(solution)/shard_map/psum | solution.py:281
  690.6 38.7 %psum.105 = bf16[32,512]{1,0:T(8,128)(2,1)S(1)} all-reduce(bf16[32,512]{1,0:T(8,128)(2,1)S(1)} %convolution_convert_fusion.1), channel_id=1, replica_groups=mesh['rows'=8,'feat'=4] {'rows'}, use_global_device_ids=true, to_apply=%region_30.31 | all-reduce | flops 16384 | bytes 65536 | tf_op jit(solution)/shard_map/psum | solution.py:279
  729.9 3.5 fusion.134
  736.1 119.7 %all-reduce.4.cloned.1.call-done = (f32[512,1536]{1,0:T(8,128)}, f32[512,512]{1,0:T(8,128)}, f32[512,1024]{1,0:T(8,128)}, f32[1024,512]{1,0:T(8,128)}) async-done(((f32[512,1536]{1,0:T(8,128)}, f32[512,512]{1,0:T(8,128)}, f32[512,1024]{1,0:T(8,128)}, f32[1024,512]{1,0:T(8,128)}), (f32[512,1536]{1,0:T(8,128)}, f32[512,512]{1,0:T(8,128)}, f32[512,1024]{1,0:T(8,128)}, ...) | async-done | bytes 8388624 | tf_op jit(solution)/shard_map/psum | solution.py:281
  855.9 3.9 copy.104
  (374 shorter events, 197.3 us)
Async XLA Ops:
  7.2 88.8 %copy-start = (bf16[512,1536]{1,0:T(8,128)(2,1)S(1)}, bf16[512,1536]{1,0:T(8,128)(2,1)}, u32[]{:S(2)}) copy-start(bf16[512,1536]{1,0:T(8,128)(2,1)} %param.30) | copy-start | bytes 4718596
  7.2 88.8 %reduce-scatter.4.cloned.1.call-start = ((), (), s32[]{:S(2)}) async-start(), calls=%async_computation.3 | async-start | bytes 10485760 | tf_op jit(solution)/shard_map/reduce_scatter | solution.py:103
  7.3 14.1 %copy-start.56 = (s32[32]{0:T(128)}, s32[32]{0:T(128)S(1)}, u32[]{:S(2)}) copy-start(s32[32]{0:T(128)S(1)} %iota_add_fusion) | copy-start | bytes 388
  8.0 13.3 %copy-start.58 = (f32[6]{0:T(128)}, f32[6]{0:T(128)S(1)}, u32[]{:S(2)}) copy-start(f32[6]{0:T(128)S(1)} %divide_sqrt_fusion) | copy-start | bytes 76
  8.9 98.0 %copy-start.36 = (s32[6,1]{0,1:T(1,128)}, s32[6,1]{0,1:T(1,128)S(1)}, u32[]{:S(2)}) copy-start(s32[6,1]{0,1:T(1,128)S(1)} %reduce-window.4) | copy-start | bytes 76
  9.6 11.7 %copy-start.38 = (s32[6]{0:T(128)}, s32[6]{0:T(128)S(1)}, u32[]{:S(2)}) copy-start(s32[6]{0:T(128)S(1)} %get-tuple-element.268) | copy-start | bytes 76
  9.6 11.7 %copy-start.48 = (f32[6]{0:T(128)}, f32[6]{0:T(128)S(1)}, u32[]{:S(2)}) copy-start(f32[6]{0:T(128)S(1)} %get-tuple-element.270) | copy-start | bytes 76
  9.8 97.1 %copy-start.33 = (f32[4096]{0:T(1024)}, f32[4096]{0:T(1024)S(1)}, u32[]{:S(2)}) copy-start(f32[4096]{0:T(1024)S(1)} %convert_reduce_fusion.8) | copy-start | bytes 49156
  13.0 8.4 copy-start.40
  21.4 74.6 %copy-start.75 = (f32[512]{0:T(512)S(1)}, f32[512]{0:T(512)}, u32[]{:S(2)}) copy-start(f32[512]{0:T(512)} %param.29) | copy-start | bytes 6148
  21.4 80.6 %copy-start.60 = (f32[512]{0:T(512)S(1)}, f32[512]{0:T(512)}, u32[]{:S(2)}) copy-start(f32[512]{0:T(512)} %param.32) | copy-start | bytes 6148
  21.4 80.6 %copy-start.61 = (f32[512]{0:T(512)S(1)}, f32[512]{0:T(512)}, u32[]{:S(2)}) copy-start(f32[512]{0:T(512)} %param.31) | copy-start | bytes 6148
  21.4 117.2 %all-gather.6.cloned.1.call-start = ((), (), s32[]{:S(2)}) async-start(), calls=%async_computation.5 | async-start | bytes 5242880 | tf_op jit(solution)/shard_map/all_gather | solution.py:118
  104.0 71.4 %all-gather.4.cloned.1.call-start = ((), (), s32[]{:S(2)}) async-start(), calls=%async_computation.4 | async-start | bytes 5242880 | tf_op jit(solution)/shard_map/all_gather | solution.py:117
  106.8 473.2 %reduce-scatter.6.cloned.1.call-start = ((), (), s32[]{:S(2)}) async-start(), calls=%async_computation.6 | async-start | bytes 5242880 | tf_op jit(solution)/shard_map/reduce_scatter | solution.py:256
  176.4 57.7 %copy-start.32 = (bf16[512,512]{1,0:T(8,128)(2,1)S(1)}, bf16[512,512]{1,0:T(8,128)(2,1)}, u32[]{:S(2)}) copy-start(bf16[512,512]{1,0:T(8,128)(2,1)} %param.33) | copy-start | bytes 1572868
  176.4 57.7 %copy-start.71 = (f32[512]{0:T(512)S(1)}, f32[512]{0:T(512)}, u32[]{:S(2)}) copy-start(f32[512]{0:T(512)} %param.34) | copy-start | bytes 6148
  176.4 57.7 %copy-start.76 = (f32[512]{0:T(512)S(1)}, f32[512]{0:T(512)}, u32[]{:S(2)}) copy-start(f32[512]{0:T(512)} %param.29) | copy-start | bytes 6148
  236.9 22.9 %copy-start.18 = (f32[1024,512]{1,0:T(8,128)}, f32[1024,512]{1,0:T(8,128)S(1)}, u32[]{:S(2)}) copy-start(f32[1024,512]{1,0:T(8,128)S(1)} %get-tuple-element.274) | copy-start | bytes 6291460
  237.0 22.9 %copy-start.42 = (f32[1024]{0:T(1024)}, f32[1024]{0:T(1024)S(1)}, u32[]{:S(2)}) copy-start(f32[1024]{0:T(1024)S(1)} %broadcast_multiply_fusion.5) | copy-start | bytes 12292
  237.4 22.4 %copy-start.44 = (f32[1024]{0:T(1024)}, f32[1024]{0:T(1024)S(1)}, u32[]{:S(2)}) copy-start(f32[1024]{0:T(1024)S(1)} %add_rsqrt_fusion.1) | copy-start | bytes 12292
  237.5 9.9 %copy-start.67 = (bf16[1024,512]{1,0:T(8,128)(2,1)S(1)}, bf16[1024,512]{1,0:T(8,128)(2,1)}, u32[]{:S(2)}) copy-start(bf16[1024,512]{1,0:T(8,128)(2,1)} %param.39) | copy-start | bytes 3145732
  237.5 9.9 %copy-start.72 = (f32[512]{0:T(512)S(1)}, f32[512]{0:T(512)}, u32[]{:S(2)}) copy-start(f32[512]{0:T(512)} %param.40) | copy-start | bytes 6148
  268.1 23.4 %copy-start.14 = (bf16[512,512]{1,0:T(8,128)(2,1)}, bf16[512,512]{1,0:T(8,128)(2,1)S(1)}, u32[]{:S(2)}) copy-start(bf16[512,512]{1,0:T(8,128)(2,1)S(1)} %dynamic-slice_bitcast_fusion.10) | copy-start | bytes 1572868 | tf_op jit(solution)/shard_map/while
  333.9 6.5 slice-start.2
  374.0 6.2 copy-start.9
  374.0 6.2 copy-start.10
  374.0 6.2 copy-start.11
  393.2 23.4 %copy-start.14 = (bf16[512,512]{1,0:T(8,128)(2,1)}, bf16[512,512]{1,0:T(8,128)(2,1)S(1)}, u32[]{:S(2)}) copy-start(bf16[512,512]{1,0:T(8,128)(2,1)S(1)} %dynamic-slice_bitcast_fusion.10) | copy-start | bytes 1572868 | tf_op jit(solution)/shard_map/while
  459.2 6.3 slice-start.2
  499.1 6.2 copy-start.9
  499.1 6.2 copy-start.10
  535.3 91.6 %reduce-scatter.8.cloned.1.call-start = ((), (), s32[]{:S(2)}) async-start(), calls=%async_computation.7 | async-start | bytes 5242880 | tf_op jit(solution)/shard_map/reduce_scatter | solution.py:259
  543.1 83.7 %copy-start.22 = (bf16[2,512,512]{2,1,0:T(8,128)(2,1)S(1)}, bf16[2,512,512]{2,1,0:T(8,128)(2,1)}, u32[]{:S(2)}) copy-start(bf16[2,512,512]{2,1,0:T(8,128)(2,1)} %get-tuple-element.131) | copy-start | bytes 3145732
  543.1 144.2 %all-gather.8.cloned.1.call-start = ((), (), s32[]{:S(2)}) async-start(), calls=%async_computation.8 | async-start | bytes 5242880 | tf_op jit(solution)/shard_map/all_gather | solution.py:274
  631.9 224.0 %all-reduce.4.cloned.1.call-start = ((), (), s32[]{:S(2)}) async-start(), calls=%async_computation.9 | async-start | bytes 16777216 | tf_op jit(solution)/shard_map/psum | solution.py:281
  645.1 42.3 %copy-start.24 = (bf16[4096,32]{0,1:T(8,128)(2,1)S(1)}, bf16[4096,32]{0,1:T(8,128)(2,1)}, u32[]{:S(2)}) copy-start(bf16[4096,32]{0,1:T(8,128)(2,1)} %copy-done.23) | copy-start | bytes 786436
  645.1 84.8 %copy-start.35 = (bf16[32,512]{1,0:T(8,128)(2,1)S(1)}, bf16[32,512]{1,0:T(8,128)(2,1)}, u32[]{:S(2)}) copy-start(bf16[32,512]{1,0:T(8,128)(2,1)} %param.28) | copy-start | bytes 98308
  690.5 43.0 %copy-start.17 = (f32[4096,32]{0,1:T(8,128)S(1)}, f32[4096,32]{0,1:T(8,128)}, u32[]{:S(2)}) copy-start(f32[4096,32]{0,1:T(8,128)} %copy-done.16) | copy-start | bytes 1572868
  690.5 43.0 %copy-start.37 = (s32[6,1]{0,1:T(1,128)S(1)}, s32[6,1]{0,1:T(1,128)}, u32[]{:S(2)}) copy-start(s32[6,1]{0,1:T(1,128)} %copy-done.36) | copy-start | bytes 76
  690.5 43.0 %copy-start.39 = (s32[6]{0:T(128)S(1)}, s32[6]{0:T(128)}, u32[]{:S(2)}) copy-start(s32[6]{0:T(128)} %copy-done.38) | copy-start | bytes 76
  690.5 43.0 %copy-start.41 = (f32[6,32]{1,0:T(8,128)S(1)}, f32[6,32]{1,0:T(8,128)}, u32[]{:S(2)}) copy-start(f32[6,32]{1,0:T(8,128)} %copy-done.40) | copy-start | bytes 2308
  690.5 43.0 %copy-start.49 = (f32[6]{0:T(128)S(1)}, f32[6]{0:T(128)}, u32[]{:S(2)}) copy-start(f32[6]{0:T(128)} %copy-done.48) | copy-start | bytes 76
  690.5 43.0 %copy-start.55 = (s32[1,6]{1,0:T(1,128)S(1)}, s32[1,6]{1,0:T(1,128)}, u32[]{:S(2)}) copy-start(s32[1,6]{1,0:T(1,128)} %param.27) | copy-start | bytes 76
  690.5 43.0 %copy-start.57 = (s32[32]{0:T(128)S(1)}, s32[32]{0:T(128)}, u32[]{:S(2)}) copy-start(s32[32]{0:T(128)} %copy-done.56) | copy-start | bytes 388
  690.5 43.0 %copy-start.59 = (f32[6]{0:T(128)S(1)}, f32[6]{0:T(128)}, u32[]{:S(2)}) copy-start(f32[6]{0:T(128)} %copy-done.58) | copy-start | bytes 76
  690.6 43.4 %copy-start.29 = (f32[4096,32]{0,1:T(8,128)S(1)}, f32[4096,32]{0,1:T(8,128)}, u32[]{:S(2)}) copy-start(f32[4096,32]{0,1:T(8,128)} %get-tuple-element.272) | copy-start | bytes 1572868
  690.6 43.4 %copy-start.34 = (f32[4096]{0:T(1024)S(1)}, f32[4096]{0:T(1024)}, u32[]{:S(2)}) copy-start(f32[4096]{0:T(1024)} %copy-done.33) | copy-start | bytes 49156
  (67 other events, 216.1 us)
Sparse Core Ops, SparseCore 0:
  21.5 74.4 reduce-scatter.3
  104.1 34.4 all-gather.5
  140.9 34.4 all-gather.3
  535.4 44.5 reduce-scatter.5
  582.3 44.4 reduce-scatter.7
  632.0 35.1 all-gather.7
  675.4 180.3 all-reduce.3
where the time goes:
time: 877 us; the launch traced here: 870 us
  waiting for transfers between devices  345 us (39%)
  matrix products  249 us (28%)
  other arithmetic  111 us (13%)
  blocking collectives  79.1 us (9%)
  local copies, waits for them, and re-layouts  61 us (7%)
  between operations  15.2 us (2%)
  loops' own time  9.72 us (1%)
    psum x1, waiting for transfers between devices, per_device(): lax.psum((grad_b_enc, grad_w_qkv, grad_b_query, grad_b_value, grad_w_out,...  120 us
    reduce_scatter x1, waiting for transfers between devices, per_device(): lax.psum_scatter(jnp.dot(normed_low, w_enc, preferred_element_type=jnp.fl...  74.5 us
    convert_element_type x8, other arithmetic, backward_block(): dscore_low = (probs * (dprobs - dprob_sum)).astype(jnp.bfloat16)  63.4 us
    dot_general x16, matrix products, head_scores(): jnp.einsum('qd,kd->qk', query_blk[:, lower:lower + HD], keys_all[:, lower...  56.4 us
    reduce_scatter x1, waiting for transfers between devices, per_device(): lax.psum_scatter(value_grad.astype(jnp.bfloat16), 'feat', scatter_dimensi...  46.9 us
    dot_general x8, matrix products, backward_block(): jnp.einsum('qd,kd->qk', grad_head, values_all[:, lower:lower + HD], prefe...  46.5 us
    psum x1, blocking collectives, per_device(): lax.psum((grad_b_enc, grad_w_qkv, grad_b_query, grad_b_value, grad_w_out,...  40.4 us
    psum x1, blocking collectives, per_device(): lax.psum(grad_w_enc_part.astype(jnp.bfloat16), 'rows').astype(jnp.float32)  38.7 us
  transfers between devices with their start and end apart: 7, of which 6 were waited for; matrix products, arithmetic and copies ran while one was open for 4% of the time, Pallas kernels for 0%

commit v1 on v0

v1 whole, which is shorter than its diff:
```python
import functools
import math

import jax
import jax.numpy as jnp
from jax import lax
from jax.experimental import pallas as pl
from jax.experimental.pallas import tpu as pltpu
from jax.sharding import PartitionSpec as P

HEADS = 4
HD = 128
FEATS = 100
EPS = 1e-5
LOG2E = 1.4426950408889634
BIG = 1e30
SLOTS = 8
VMEM_BYTES = 58 * 1024 * 1024

BF = jnp.bfloat16
F32 = jnp.float32
MESH = pl.DeviceIdType.MESH


def dot(a, b):
    return lax.dot_general(a, b, (((1,), (0,)), ((), ())), preferred_element_type=F32)


def dot_nt(a, b):
    return lax.dot_general(a, b, (((1,), (1,)), ((), ())), preferred_element_type=F32)


def dot_tn(a, b):
    return lax.dot_general(a, b, (((0,), (0,)), ((), ())), preferred_element_type=F32)


def split3(v):
    high = v.astype(BF)
    rest = v - high.astype(F32)
    mid = rest.astype(BF)
    return high, mid, (rest - mid.astype(F32)).astype(BF)


def dot_split(v, b):
    high, mid, small = split3(v)
    return dot(high, b) + dot(mid, b) + dot(small, b)


def aug_lanes(base, value):
    high, mid, small = (part.astype(F32) for part in split3(value))
    lane = lax.broadcasted_iota(jnp.int32, base.shape, 1)
    out = jnp.where(lane == SLOTS, high, base.astype(F32))
    out = jnp.where(lane == SLOTS + 1, mid, out)
    return jnp.where(lane == SLOTS + 2, small, out).astype(BF)

def bits_below(count):
    return [1 << i for i in range(count.bit_length() - 1)]


def bit_of(index, bit):
    return lax.rem(index // bit, 2)


def flip(index, bit):
    return index + bit * (1 - 2 * bit_of(index, bit))


def greet(peers):
    barrier = pltpu.get_barrier_semaphore()
    for peer in peers:
        pl.semaphore_signal(barrier, inc=1, device_id=peer, device_id_type=MESH)
    pl.semaphore_wait(barrier, len(peers))


def send(src, dst, sems, slot, peer):
    return pltpu.make_async_remote_copy(
        src_ref=src, dst_ref=dst, send_sem=sems[0].at[slot], recv_sem=sems[1].at[slot],
        device_id=peer, device_id_type=MESH,
    )


def gather_feat(mine, full, sems, first, feat_count):
    me = lax.axis_index("feat")
    block = mine.shape[0]

    def at(index):
        return full.at[pl.ds(pl.multiple_of(index * block, block), block)]

    order = bits_below(feat_count)[::-1]
    steps = []
    held = [()]
    for bit in order:
        for path in held:
            steps.append((path, bit))
        held = held + [path + (bit,) for path in held]

    def make(number):
        path, bit = steps[number]
        index = me
        for done in path:
            index = flip(index, done)
        src = mine if not path else at(index)
        return send(src, at(index), sems, first + number, {"feat": flip(me, bit)})

    own = [n for n, (path, _) in enumerate(steps) if not path]
    for number in own:
        make(number).start()

    def finish():
        full[pl.ds(pl.multiple_of(me * block, block), block), :] = mine[...]
        for number, (path, _) in enumerate(steps):
            if path:
                make(number).start()
            make(number).wait_recv()
        for number in range(len(steps)):
            make(number).wait_send()

    return finish, len(steps)


def chunked(items, size):
    return [items[i : i + size] for i in range(0, len(items), size)]


class AllReduce:
    def __init__(self, x, out, work, first_in, later_in, sems, places, parts, group):
        self.x, self.out, self.work = x, out, work
        self.first_in, self.later_in, self.sems = first_in, later_in, sems
        self.place = {axis: lax.axis_index(axis) for axis in places}
        self.core = bit_of(self.place["feat"], 1)
        groups = chunked(reduce_bits(places), group)
        self.depth = len(groups)
        self.parts = []
        self.count = 2
        start = 0
        for number, size in enumerate(parts):
            turn = number * len(groups) // len(parts)
            at, landing, levels = start, start, []
            length = size
            for bits in groups[turn:] + groups[:turn]:
                length = length // 2 ** len(bits)
                member = sum(self.bit(b) << i for i, b in enumerate(bits))
                peers = []
                for subset in range(1, 2 ** len(bits)):
                    theirs = member
                    where = dict(self.place)
                    for i, (axis, bit) in enumerate(bits):
                        if subset >> i & 1:
                            theirs = theirs + (1 - 2 * self.bit((axis, bit))) * 2**i
                            where[axis] = flip(where[axis], bit)
                    peers.append((where, at + theirs * length, landing, self.count))
                    landing += length
                    self.count += 2
                at = at + member * length
                levels.append((peers, at, length))
            self.parts.append(levels)
            start += size

    def bit(self, which):
        return bit_of(self.place[which[0]], which[1])

    def rows(self, at, size):
        return pl.ds(pl.multiple_of(at, 16), size)

    def core_in(self):
        return send(self.x.at[1 - self.core], self.first_in, self.sems, 0, self.peers()[0])

    def core_out(self):
        half = self.out.at[self.core]
        return send(half, half, self.sems, 1, self.peers()[0])

    def down(self, part, level):
        peers, _, size = self.parts[part][level]
        return [
            send(
                self.work.at[self.rows(at, size)], self.later_in.at[pl.ds(landing, size)],
                self.sems, slot, where,
            )
            for where, at, landing, slot in peers
        ]

    def up(self, part, level):
        peers, at, size = self.parts[part][level]
        seg = self.out.at[self.core, self.rows(at, size)]
        return [send(seg, seg, self.sems, slot + 1, where) for where, _, _, slot in peers]

    def stage(self, number):
        depth = self.depth
        everyone = range(len(self.parts))
        if number == 0:
            self.core_in().start()
        elif number == 1:
            self.core_in().wait()
            total = self.x[self.core].astype(F32) + self.first_in[...].astype(F32)
            self.work[...] = total.astype(BF)
            for part in everyone:
                start_all(self.down(part, 0))
        elif number <= depth + 1:
            level = number - 2
            for part in everyone:
                wait_all(self.down(part, level))
                peers, at, size = self.parts[part][level]
                total = self.work[self.rows(at, size), :].astype(F32)
                for _, _, landing, _ in peers:
                    total = total + self.later_in[landing : landing + size, :].astype(F32)
                if level + 1 < depth:
                    self.work[self.rows(at, size), :] = total.astype(BF)
                    start_all(self.down(part, level + 1))
                else:
                    self.out[self.core, self.rows(at, size), :] = total.astype(BF)
                    start_all(self.up(part, level))
        elif number <= 2 * depth + 1:
            level = depth - 1 - (number - depth - 2)
            for part in everyone:
                wait_all(self.up(part, level))
                if level > 0:
                    start_all(self.up(part, level - 1))
            if level == 0:
                self.core_out().start()
        else:
            self.core_out().wait()

    @property
    def stages(self):
        return 2 * self.depth + 3

    def peers(self):
        first = dict(self.place)
        first["feat"] = flip(first["feat"], 1)
        return [first] + [where for peers, _, _ in self.parts[0] for where, _, _, _ in peers]


def start_all(copies):
    for copy in copies:
        copy.start()


def wait_all(copies):
    for copy in copies:
        copy.wait()


def reduce_bits(places):
    return [("feat", b) for b in bits_below(places["feat"])[1:]] + [
        ("rows", b) for b in bits_below(places["rows"])
    ]


def reduce_plan(rows_needed, places, group):
    bits = reduce_bits(places)
    groups = chunked(bits, group)
    granule = 16 * 2 ** len(bits)
    units = -(-rows_needed // granule)
    first = -(-units * 2 // 3)
    parts = [first, units - first] if len(groups) > 1 and units > 1 else [units]
    parts = [size * granule for size in parts]
    sems = 2 + 2 * len(parts) * sum(2 ** len(g) - 1 for g in groups)
    landing = sum(parts)
    return sum(parts), parts, sems, landing


def tail_kernel(
    x, grad, features_t, memt, trt, tab, stats,
    out, grad_x,
    mine, held, grad_in, work, first_in, later_in, send_s, recv_s, gsend_s, grecv_s,
    *, places, parts, group,
):
    me = lax.axis_index("feat")
    feat_count = places["feat"]
    reduce = AllReduce(
        x, out, work, first_in, later_in, (send_s, recv_s), places, parts, group
    )
    greet(reduce.peers())
    order = bits_below(feat_count)
    slots, number = {}, 0
    for bit in order:
        for i in range(feat_count // (2 * bit)):
            slots[bit, i] = number
            number += 1

    def copy(bit, i):
        j = 1 - bit_of(me, bit) + 2 * i
        src = grad.at[j] if bit == 1 else held.at[slots[bit // 2, 0] + j]
        return send(
            src, grad_in.at[slots[bit, i]], (gsend_s, grecv_s), slots[bit, i],
            {"feat": flip(me, bit)},
        )

    for i in range(feat_count // 2):
        copy(1, i).start()
    reduce.stage(0)
    for level, bit in enumerate(order):
        for i in range(feat_count // (2 * bit)):
            copy(bit, i).wait()
            j = bit_of(me, bit) + 2 * i
            here = grad[j] if bit == 1 else held[slots[bit // 2, 0] + j]
            total = here.astype(F32) + grad_in[slots[bit, i]].astype(F32)
            if level + 1 < len(order):
                held[slots[bit, i]] = total.astype(BF)
            else:
                mine[...] = total
        if level + 1 < len(order):
            for i in range(feat_count // (4 * bit)):
                copy(2 * bit, i).start()
        if level == 0:
            reduce.stage(1)

    cols_mine, rows = features_t.shape
    mean, var, factor = (stats[i, pl.ds(pl.multiple_of(me * cols_mine, 8), cols_mine), :] for i in range(3))
    count = tab[0:1, :]
    step = 512
    pieces = [slice(at, at + step) for at in range(0, rows, step)]

    def gather(v, member):
        high, mid, small = split3(v)
        return dot_nt(high, member) + dot_nt(mid, member) + dot_nt(small, member)

    d_factor = jnp.zeros((cols_mine, SLOTS), F32)
    for cut in pieces:
        c = features_t[:, cut].astype(F32) - dot_split(mean, memt[:, cut])
        grad_x[:, cut] = c
        d_factor = d_factor + gather(mine[:, cut] * c, memt[:, cut])
    reduce.stage(2)
    side = jnp.where(var > 0.25, 1.0, jnp.where(var == 0.25, 0.5, 0.0))
    d_var = d_factor * (-0.5) * factor / jnp.maximum(var, 0.25) * side
    pull = 2.0 * d_var / count
    d_mean = jnp.zeros((cols_mine, SLOTS), F32)
    for cut in pieces:
        dc = mine[:, cut] * dot_split(factor, memt[:, cut]) + grad_x[:, cut] * dot_split(
            pull, trt[:, cut]
        )
        grad_x[:, cut] = dc
        d_mean = d_mean - gather(dc, memt[:, cut])
    reduce.stage(3)
    d_mean = d_mean / count
    for cut in pieces:
        grad_x[:, cut] = grad_x[:, cut] + dot_split(d_mean, trt[:, cut])
    for number in range(4, reduce.stages):
        reduce.stage(number)


def prep_kernel(
    x_mine, w_mine, memt, trt, tab, b_enc, w_qkv, b_query, b_value,
    w_enc, stats, normed, normed_t, w_low, keys, vals, query, enc,
    xt, w_pair, cent, send_s, recv_s, *, rows_mine, feat_count,
):
    me = lax.axis_index("feat")
    greet([{"feat": flip(me, bit)} for bit in bits_below(feat_count)])
    end_x, used = gather_feat(x_mine, xt, (send_s, recv_s), 0, feat_count)
    end_w, _ = gather_feat(w_mine, w_enc, (send_s, recv_s), used, feat_count)
    columns, rows = xt.shape
    width = w_enc.shape[1]
    end_w()
    w_prod = dot(w_enc[...], w_qkv[...])
    high, mid, _ = split3(w_prod)
    w_pair[0:columns, :] = high
    w_pair[columns:, :] = mid
    w_low[...] = high
    bias = dot_split(jnp.broadcast_to(b_enc[...], (8, width)), w_qkv[...])[0:1, :]
    end_x()
    step = 512
    row_lo = pl.multiple_of(lax.axis_index("feat") * rows_mine, rows_mine)
    count = tab[0:1, :]
    sums = jnp.zeros((columns, SLOTS), F32)
    for at in range(0, rows, step):
        sums = sums + dot_nt(xt[:, at : at + step], trt[:, at : at + step])
    mean = sums / count
    var = jnp.zeros((columns, SLOTS), F32)
    for at in range(0, rows, step):
        member = memt[:, at : at + step]
        train = trt[:, at : at + step]
        c = xt[:, at : at + step].astype(F32) - dot_split(mean, member)
        cent[:, at : at + step] = c
        sq = c * c
        high, mid, _ = split3(sq)
        var = var + (dot_nt(high, train) + dot_nt(mid, train))
    var = var / count
    column = lax.broadcasted_iota(jnp.int32, (columns, SLOTS), 0).astype(F32)
    keep = column < tab[2:3, :]
    factor = jnp.where(keep, lax.rsqrt(jnp.maximum(var, 0.25)) * tab[1:2, :], 0.0)
    stats[0] = mean
    stats[1] = var
    stats[2] = factor

    for at in range(0, rows, step):
        member = memt[:, at : at + step]
        nt = cent[:, at : at + step] * dot_split(factor, member)
        normed_t[:, at : at + step] = nt.astype(BF)
        n = nt.T.astype(BF)
        normed[at : at + step, :] = n
        both = jnp.concatenate([n, n], axis=1)
        keys[at : at + step, :] = (
            dot(both, w_pair[:, width : 2 * width]) + bias[:, width : 2 * width]
        ).astype(BF)
        vals[at : at + step, :] = (
            dot(both, w_pair[:, 2 * width :]) + (bias[:, 2 * width :] + b_value[...])
        ).astype(BF)
    scale = LOG2E / math.sqrt(HD)
    step = min(256, rows_mine)
    for at in range(0, rows_mine, step):
        n = normed[pl.ds(row_lo + at, step), :]
        both = jnp.concatenate([n, n], axis=1)
        query[at : at + step, :] = (
            (dot(both, w_pair[:, 0:width]) + (bias[:, 0:width] + b_query[...])) * scale
        ).astype(BF)
        enc[at : at + step, :] = dot(n, w_enc[...]) + b_enc[...]


def tile_lanes(v, wide):
    return jnp.concatenate([v] * (wide // v.shape[1]), axis=1)


def forward_kernel(query, keys, vals, key_aug, query_tab, att, query_aug, acc, peak):
    rows_mine = query.shape[0]
    rows = keys.shape[0]
    q_step = min(256, rows_mine)
    k_step = 512
    ones = jnp.ones((k_step, HD), BF)

    @pl.loop(0, rows_mine // q_step)
    def _(block):
        q_rows = pl.ds(pl.multiple_of(block * q_step, q_step), q_step)
        table = query_tab[q_rows, :]
        for head in range(HEADS):
            acc[head] = jnp.zeros((q_step, 2 * HD), F32)
            peak[head] = jnp.full((q_step, HD), -3e38, F32)

        @pl.loop(0, rows // k_step)
        def _(chunk):
            k_rows = pl.ds(pl.multiple_of(chunk * k_step, k_step), k_step)
            aug = key_aug[k_rows, :]
            for head in range(HEADS):
                lanes = slice(head * HD, (head + 1) * HD)
                q = jnp.concatenate([query[q_rows, lanes], table], axis=1)
                k = jnp.concatenate([keys[k_rows, lanes], aug], axis=1)
                s = dot_nt(q, k)
                old = peak[head]
                new = jnp.maximum(old, jnp.max(s, axis=1, keepdims=True))
                peak[head] = new
                p = jnp.exp2(s - tile_lanes(new, k_step)).astype(BF)
                v = jnp.concatenate([vals[k_rows, lanes], ones], axis=1)
                alpha = tile_lanes(jnp.exp2(old - new), 2 * HD)
                acc[head] = acc[head] * alpha + dot(p, v)

        for head in range(HEADS):
            lanes = slice(head * HD, (head + 1) * HD)
            total = acc[head]
            norm = total[:, HD:]
            att[q_rows, lanes] = total[:, :HD] / norm
            query_aug[head, q_rows, :] = aug_lanes(table, -(peak[head] + jnp.log2(norm)))


def ffn_kernel(
    enc, att, normed, cot, w_out, b_out, gain_one, shift_one, w_up, b_up, w_down, b_down,
    gain_two, shift_two,
    out, grad_res, grad_att, att_aug, packed,
    small, attl_s, gbl_s, o1_s, gpre_s, act_s, gffn_s, nm_s, *, rows_mine,
):
    width = enc.shape[1]
    hidden = w_up.shape[1]
    step = min(256, rows_mine)
    row_lo = pl.multiple_of(lax.axis_index("feat") * rows_mine, rows_mine)
    small[...] = jnp.zeros(small.shape, F32)

    def add_small(slot, value, wide):
        small[slot : slot + 1, 0:wide] += jnp.sum(value, axis=0, keepdims=True)

    @pl.loop(0, rows_mine // step)
    def _(block):
        rows = pl.ds(pl.multiple_of(block * step, step), step)
        attended = att[rows, :]
        attl = attended.astype(BF)
        attl_s[rows, :] = attl
        resid = enc[rows, :] + dot(attl, w_out[...]) + b_out[...]
        ctr = resid - jnp.mean(resid, axis=1, keepdims=True)
        rstd1 = lax.rsqrt(jnp.mean(ctr * ctr, axis=1, keepdims=True) + EPS)
        n1 = ctr * rstd1
        o1 = n1 * gain_one[...] + shift_one[...]
        o1l = o1.astype(BF)
        o1_s[rows, :] = o1l
        pre = dot(o1l, w_up[...]) + b_up[...]
        cdf = 0.5 + 0.5 * lax.erf(pre * (1.0 / math.sqrt(2.0)))
        slope = cdf + pre * (jnp.exp(-0.5 * pre * pre) * (1.0 / math.sqrt(2.0 * math.pi)))
        actl = (pre * cdf).astype(BF)
        act_s[rows, :] = actl
        r2 = o1 + dot(actl, w_down[...]) + b_down[...]
        ctr2 = r2 - jnp.mean(r2, axis=1, keepdims=True)
        rstd2 = lax.rsqrt(jnp.mean(ctr2 * ctr2, axis=1, keepdims=True) + EPS)
        n2 = ctr2 * rstd2
        out[rows, :] = (n2 * gain_two[...] + shift_two[...]).astype(BF)
        go = cot[rows, :].astype(F32)
        add_small(0, go * n2, width)
        add_small(1, go, width)
        dn = go * gain_two[...]
        g2 = rstd2 * (
            dn - jnp.mean(dn, axis=1, keepdims=True) - n2 * jnp.mean(dn * n2, axis=1, keepdims=True)
        )
        gfl = g2.astype(BF)
        gffn_s[rows, :] = gfl
        add_small(2, g2, width)
        gpl = (dot_nt(gfl, w_down[...]) * slope).astype(BF)
        gpre_s[rows, :] = gpl
        add_small(3, gpl.astype(F32), hidden)
        g1 = dot_nt(gpl, w_up[...]) + g2
        add_small(4, g1 * n1, width)
        add_small(5, g1, width)
        dn1 = g1 * gain_one[...]
        gr = rstd1 * (
            dn1 - jnp.mean(dn1, axis=1, keepdims=True)
            - n1 * jnp.mean(dn1 * n1, axis=1, keepdims=True)
        )
        add_small(6, gr, width)
        gbl = gr.astype(BF)
        gbl_s[rows, :] = gbl
        grad_res[rows, :] = gbl
        ga = dot_nt(gbl, w_out[...]).astype(BF)
        grad_att[rows, :] = ga
        prod = ga.astype(F32) * attended
        zero = jnp.zeros((step, HD), BF)
        for head in range(HEADS):
            lanes = slice(head * HD, (head + 1) * HD)
            row_sum = jnp.sum(prod[:, lanes], axis=1, keepdims=True)
            att_aug[head, rows, :] = aug_lanes(zero, jnp.broadcast_to(-row_sum, (step, HD)))

    nm_s[...] = normed[pl.ds(row_lo, rows_mine), :]
    tile = 256
    half = width // 2

    def pack(at, value):
        rows = slice(at, at + value.shape[0])
        packed[0, rows, :] = value[:, :half].astype(BF)
        packed[1, rows, :] = value[:, half:].astype(BF)

    for at in range(0, width, tile):
        cut = slice(at, at + tile)
        pack(at, dot_tn(attl_s[:, cut], gbl_s[...]))
    base = width
    for at in range(0, width, tile):
        cut = slice(at, at + tile)
        up = dot_tn(o1_s[:, cut], gpre_s[...])
        for part in range(hidden // width):
            pack(base + part * width + at, up[:, part * width : (part + 1) * width])
    base = base + hidden
    for at in range(0, hidden, tile):
        cut = slice(at, at + tile)
        pack(base + at, dot_tn(act_s[:, cut], gffn_s[...]))
    base = base + hidden
    pack(base, dot_tn(nm_s[...], gbl_s[...]))
    base = base + normed.shape[1]
    pack(base, jnp.concatenate([small[:, :width], small[:, width:]], axis=0))
    base = base + 16
    if base < packed.shape[1]:
        packed[:, base:, :] = jnp.zeros((2, packed.shape[1] - base, half), BF)


def backward_kernel(
    query, query_aug, grad_att, att_aug, keys, vals, key_aug, normed_t, w_low, w_enc, grad_res,
    early, grad_low, late, early_out,
    grad_normed, moment, colsum, dq, dkv, work, first_in, later_in, send_s, recv_s,
    *, rows_mine, places, parts, group,
):
    reduce = AllReduce(
        early, early_out, work, first_in, later_in, (send_s, recv_s), places, parts, group
    )
    greet(reduce.peers())
    rows, width = keys.shape
    columns = normed_t.shape[0]
    k_step = 512
    slots = (0, 1, 5, 8, 11, 15)
    slots = slots[: min(len(slots), reduce.stages)]
    row_lo = pl.multiple_of(lax.axis_index("feat") * rows_mine, rows_mine)
    dq[...] = jnp.zeros(dq.shape, F32)
    moment[...] = jnp.zeros(moment.shape, F32)
    colsum[...] = jnp.zeros(colsum.shape, F32)

    @pl.loop(0, rows // k_step)
    def _(chunk):
        k_rows = pl.ds(pl.multiple_of(chunk * k_step, k_step), k_step)
        aug = key_aug[k_rows, :]
        for head in range(HEADS):
            lanes = slice(head * HD, (head + 1) * HD)
            q = query[:, lanes]
            k = keys[k_rows, lanes]
            do = grad_att[:, lanes]
            s = dot_nt(
                jnp.concatenate([k, aug], axis=1),
                jnp.concatenate([q, query_aug[head]], axis=1),
            )
            p = jnp.exp2(s)
            dp = dot_nt(
                jnp.concatenate([vals[k_rows, lanes], aug], axis=1),
                jnp.concatenate([do, att_aug[head]], axis=1),
            )
            ds = (p * dp).astype(BF)
            dv = dot(p.astype(BF), do)
            dk = dot(ds, q) * (1.0 / LOG2E)
            dkv[:, lanes] = dk.astype(BF)
            dkv[:, width + head * HD : width + (head + 1) * HD] = dv.astype(BF)
            colsum[0:1, width + head * HD : width + (head + 1) * HD] += jnp.sum(
                dk, axis=0, keepdims=True
            )
            colsum[0:1, 2 * width + head * HD : 2 * width + (head + 1) * HD] += jnp.sum(
                dv, axis=0, keepdims=True
            )
            dq[:, lanes] += dot_tn(ds, k)
            if head % 2 == 1:
                for number, when in enumerate(slots):

                    @pl.when(2 * chunk + head // 2 == when)
                    def _(number=number):
                        reduce.stage(number)

        grads = dkv[...]
        moment[:, width:] += dot(normed_t[:, k_rows], grads)
        grad_normed[:, k_rows] = dot_nt(w_low[:, width:], grads)

    dql = (dq[...] * (1.0 / math.sqrt(HD))).astype(BF)
    mine = pl.ds(row_lo, rows_mine)
    colsum[0:1, 0:width] = jnp.sum(dql.astype(F32), axis=0, keepdims=True)
    moment[:, 0:width] = dot(normed_t[:, mine], dql)
    grad_normed[:, mine] += dot_nt(w_low[:, 0:width], dql) + dot_nt(w_enc[...], grad_res[...])
    grad_low[...] = grad_normed[...].astype(BF)
    half = width // 2
    late[...] = jnp.zeros(late.shape, BF)
    for part in range(3):
        for side in range(2):
            lanes = slice(part * width + side * half, part * width + (side + 1) * half)
            late[side, part * columns : (part + 1) * columns, :] = moment[:, lanes].astype(BF)
            at = 3 * columns + 16 * part
            late[side, at : at + 16, :] = jnp.concatenate(
                [colsum[:, lanes], jnp.zeros((8, half), F32)], axis=0
            ).astype(BF)
    for number in range(len(slots), reduce.stages):
        reduce.stage(number)


def vmem(count):
    return [pl.BlockSpec(memory_space=pltpu.VMEM)] * count


def call(kernel, outs, scratch, args, **params):
    return pl.pallas_call(
        kernel,
        out_shape=tuple(jax.ShapeDtypeStruct(shape, kind) for shape, kind in outs),
        in_specs=vmem(len(args)),
        out_specs=tuple(vmem(len(outs))),
        scratch_shapes=[
            pltpu.SemaphoreType.DMA((entry,)) if isinstance(entry, int) else pltpu.VMEM(*entry)
            for entry in scratch
        ],
        compiler_params=pltpu.CompilerParams(vmem_limit_bytes=VMEM_BYTES, **params),
    )(*args)


def per_device(
    features, lengths, train_counts, used_features, w_enc, b_enc, w_qkv, b_query, b_value,
    w_out, b_out, gain_one, shift_one, w_up, b_up, w_down, b_down, gain_two, shift_two, cotangent,
):
    feat_count = lax.axis_size("feat")
    feat_index = lax.axis_index("feat")
    rows, cols_mine = features.shape
    columns = cols_mine * feat_count
    width = w_qkv.shape[0]
    hidden = w_up.shape[1]
    rows_mine = rows // feat_count
    tables = lengths.shape[1]

    def pad(v, fill):
        return jnp.pad(v, ((0, SLOTS - tables),), constant_values=fill)

    table_len, train_count, used = lengths[0], train_counts[0], used_features[0]
    ends = jnp.cumsum(table_len)
    starts = pad(ends - table_len, rows)
    stops = pad(ends, rows)
    learned = pad(ends - table_len + train_count, rows)
    at = jnp.arange(rows, dtype=jnp.int32)[None, :]
    member = (at >= starts[:, None]) & (at < stops[:, None])
    train = member & (at < learned[:, None])
    mem_t = member.astype(BF)
    tr_t = train.astype(BF)
    used_f = pad(used, 1).astype(F32)
    tab = jnp.stack(
        [pad(train_count, 1).astype(F32), jnp.sqrt(FEATS / used_f), pad(used, 0).astype(F32)]
        + [jnp.zeros((SLOTS,), F32)] * 5
    )
    key_aug = jnp.concatenate(
        [
            jnp.where(train.T, 0.0, -BIG).astype(BF),
            jnp.ones((rows, 3), BF),
            jnp.zeros((rows, HD - SLOTS - 3), BF),
        ],
        axis=1,
    )
    query_tab = jnp.pad(
        lax.dynamic_slice_in_dim(mem_t, feat_index * rows_mine, rows_mine, axis=1).T,
        ((0, 0), (0, HD - SLOTS)),
    )

    features_t = features.T
    places = {"feat": feat_count, "rows": lax.axis_size("rows")}
    half = width // 2

    row = lambda v: v.reshape(1, -1)
    gather_sems = 2 * (feat_count - 1)
    w_enc_all, stats, normed, normed_t, w_low, keys, vals, query, enc = call(
        functools.partial(prep_kernel, rows_mine=rows_mine, feat_count=feat_count),
        [
            ((columns, width), BF), ((3, columns, SLOTS), F32), ((rows, columns), BF),
            ((columns, rows), BF), ((columns, 3 * width), BF), ((rows, width), BF),
            ((rows, width), BF), ((rows_mine, width), BF), ((rows_mine, width), F32),
        ],
        [
            ((columns, rows), BF), ((2 * columns, 3 * width), BF), ((columns, rows), F32),
            gather_sems, gather_sems,
        ],
        (features_t, w_enc, mem_t, tr_t, tab, row(b_enc), w_qkv, row(b_query), row(b_value)),
        collective_id=0, has_side_effects=True,
    )
    q_step = min(256, rows_mine)
    att, query_aug = call(
        forward_kernel,
        [((rows_mine, width), F32), ((HEADS, rows_mine, HD), BF)],
        [((HEADS, q_step, 2 * HD), F32), ((HEADS, q_step, HD), F32)],
        (query, keys, vals, key_aug, query_tab),
    )
    early_rows, early_parts, early_sems, early_land = reduce_plan(
        width + 2 * hidden + columns + 16, places, 2
    )
    out, grad_res, grad_att, att_aug, early = call(
        functools.partial(ffn_kernel, rows_mine=rows_mine),
        [
            ((rows_mine, width), BF), ((rows_mine, width), BF), ((rows_mine, width), BF),
            ((HEADS, rows_mine, HD), BF), ((2, early_rows, half), BF),
        ],
        [
            ((8, hidden), F32),
            ((rows_mine, width), BF), ((rows_mine, width), BF), ((rows_mine, width), BF),
            ((rows_mine, hidden), BF), ((rows_mine, hidden), BF), ((rows_mine, width), BF),
            ((rows_mine, columns), BF),
        ],
        (
            enc, att, normed, cotangent, w_out, row(b_out), row(gain_one), row(shift_one), w_up,
            row(b_up), w_down, row(b_down), row(gain_two), row(shift_two),
        ),
    )
    late_rows, late_parts, late_sems, late_land = reduce_plan(3 * columns + 48, places, 4)
    grad_low, late, early = call(
        functools.partial(
            backward_kernel, rows_mine=rows_mine, places=places, parts=early_parts, group=2
        ),
        [((columns, rows), BF), ((2, late_rows, half), BF), ((2, early_rows, half), BF)],
        [
            ((columns, rows), F32), ((columns, 3 * width), F32), ((8, 3 * width), F32),
            ((rows_mine, width), F32), ((512, 2 * width), BF), ((early_rows, half), BF),
            ((early_rows, half), BF), ((early_land, half), BF), early_sems, early_sems,
        ],
        (
            query, query_aug, grad_att, att_aug, keys, vals, key_aug, normed_t, w_low, w_enc_all,
            grad_res, early,
        ),
        collective_id=1, has_side_effects=True,
    )
    late, grad_x = call(
        functools.partial(
            tail_kernel, places=places, parts=late_parts, group=4
        ),
        [((2, late_rows, half), BF), ((cols_mine, rows), F32)],
        [
            ((cols_mine, rows), F32), ((feat_count - 1, cols_mine, rows), BF),
            ((feat_count - 1, cols_mine, rows), BF), ((late_rows, half), BF),
            ((late_rows, half), BF), ((late_land, half), BF), late_sems, late_sems, feat_count - 1,
            feat_count - 1,
        ],
        (
            late, grad_low.reshape(feat_count, cols_mine, rows), features_t, mem_t, tr_t, tab,
            stats,
        ),
        collective_id=2, has_side_effects=True,
    )
    grad_features = grad_x.T

    def take(v, lo, count):
        return jnp.concatenate([v[0, lo : lo + count], v[1, lo : lo + count]], axis=1)

    base = width
    grad_w_out = take(early, 0, width).astype(F32)
    grad_w_up = jnp.concatenate(
        [take(early, base + i * width, width) for i in range(hidden // width)], axis=1
    ).astype(F32)
    base = base + hidden
    grad_w_down = take(early, base, hidden).astype(F32)
    base = base + hidden
    local = take(early, base, columns).astype(F32)
    small = take(early, base + columns, 16).astype(F32)
    moment = jnp.concatenate([take(late, i * columns, columns) for i in range(3)], axis=1)
    sums = jnp.concatenate([take(late, 3 * columns + 16 * i, 1)[0] for i in range(3)]).astype(F32)
    grad_w_qkv = (
        jnp.einsum("fe,fo->eo", w_enc_all, moment, preferred_element_type=F32)
        + b_enc[:, None] * sums[None, :]
    )
    grad_w_enc = lax.dynamic_slice_in_dim(
        jnp.einsum("fo,eo->fe", moment, w_qkv, preferred_element_type=F32) + local,
        feat_index * cols_mine, cols_mine, axis=0,
    )
    grad_b_enc = (
        jnp.einsum("o,eo->e", sums, w_qkv.astype(F32), precision=lax.Precision.HIGHEST) + small[6]
    )
    return (
        out, grad_features, grad_w_enc, grad_b_enc, grad_w_qkv, sums[:width], sums[2 * width :],
        grad_w_out, small[6], small[4], small[5], grad_w_up,
        jnp.concatenate([small[3], small[11]]), grad_w_down, small[2], small[0], small[1],
    )


def solution(mesh):
    whole = P()
    in_specs = (
        (P("rows", "feat"),) + (P("rows", None),) * 3 + (P("feat", None),) + (whole,) * 14
        + (P(("rows", "feat"), None),)
    )
    out_specs = (
        (P(("rows", "feat"), None), P("rows", "feat"), P("feat", None)) + (whole,) * 14
    )
    return jax.shard_map(
        per_device, mesh=mesh, in_specs=in_specs, out_specs=out_specs, check_vma=False
    )
```

time: 877 us -> 218 us (0.25)
  waiting for transfers between devices: 345 us -> 0 us
  matrix products: 249 us -> 4.1 us
  Pallas kernels: 0 us -> 186 us
  other arithmetic: 111 us -> 13.1 us
  blocking collectives: 79.1 us -> 0 us
  local copies, waits for them, and re-layouts: 61 us -> 13.4 us
  between operations: 15.2 us -> 0.81 us
  loops' own time: 9.72 us -> 0 us
    dot_general x79 -> x3, matrix products: 249 us -> 4.1 us  [the longest x1 2.27 us: per_device(): jnp.einsum('fe,fo->eo', w_enc_all, moment, preferred_element_type=F32)]
    pallas_call x0 -> x5, Pallas kernels: none -> 186 us  [call(): pl.pallas_call(kernel, out_shape=tuple((jax.ShapeDtypeStruct(shape, kind)...]
    reduce_scatter x3 -> x0, waiting for transfers between devices: 158 us -> none  [the longest x1 74.5 us: per_device(): lax.psum_scatter(jnp.dot(normed_low, w_enc, preferred_element_type=jnp.fl...]
    psum x1 -> x0, waiting for transfers between devices: 120 us -> none  [per_device(): lax.psum((grad_b_enc, grad_w_qkv, grad_b_query, grad_b_value, grad_w_out,...]
    psum x2 -> x0, blocking collectives: 79.1 us -> none  [the longest x1 40.4 us: per_device(): lax.psum((grad_b_enc, grad_w_qkv, grad_b_query, grad_b_value, grad_w_out,...]
    all_gather x3 -> x0, waiting for transfers between devices: 67 us -> none  [the longest x1 36.7 us: per_device(): lax.all_gather(key_low, 'feat', axis=0, tiled=True)]
    convert_element_type x10 -> x8, other arithmetic: 66 us -> 6.2 us  [the longest x1 1.61 us: per_device(): grad_w_down = take(early, base, hidden).astype(F32)]
    while x82 -> x0, local copies, waits for them, and re-layouts: 31.8 us -> none
  transfers between devices with their start and end apart: 7 -> 0, of which waited for: 6 -> 0; matrix products, arithmetic and copies ran while one was open for 4% -> 0% of each run, Pallas kernels for 0% -> 0%
where the time goes in v1:
time: 218 us; the launch traced here: 217 us
  Pallas kernels  186 us (85%)
  local copies, waits for them, and re-layouts  13.4 us (6%)
  other arithmetic  13.1 us (6%)
  matrix products  4.1 us (2%)
    pallas_call x5, Pallas kernels, call(): pl.pallas_call(kernel, out_shape=tuple((jax.ShapeDtypeStruct(shape, kind)...  186 us
    unnamed x24, local copies, waits for them, and re-layouts  7.33 us

profile of v1, /device:TPU:0, one launch (start us, length us, event | category | flops | bytes accessed | tf_op | source)
XLA Modules:
  0.0 217.0 jit_solution(14591197848391737973)
XLA Ops:
  0.7 0.8 reduce-window.9
  1.5 0.7 bitcast_add_fusion
  2.2 0.8 fusion.4
  2.9 0.7 convert_bitcast_fusion
  3.6 0.7 sqrt_bitcast_fusion
  4.3 0.6 stack.19.tab
  4.9 27.8 %shard_map.323 = (bf16[128,512]{1,0:T(8,128)(2,1)}, f32[3,128,8]{2,1,0:T(8,128)}, bf16[4096,128]{1,0:T(8,128)(2,1)}, bf16[128,4096]{1,0:T(8,128)(2,1)}, bf16[128...) custom-call(bf16[32,4096]{1,0:T(8,128)(2,1)} %bitcast.94, ...), custom_call_target="tpu_custom_call" | custom-call | tf_op jit(solution)/shard_map/pallas_call | solution.py:642
  32.7 0.7 dynamic-slice_bitcast_fusion
  33.5 0.2 copy.38
  33.6 0.8 pad.29.clone.query_tab
  34.4 0.5 select_convert_fusion
  34.9 0.1 pad.54.clone
  35.0 0.1 pad.55.clone
  35.1 1.3 maximum_maximum_fusion.key_aug
  36.4 40.4 %shard_map.324 = (f32[1024,512]{1,0:T(8,128)}, bf16[4,1024,128]{2,1,0:T(8,128)(2,1)}) custom-call(bf16[1024,512]{1,0:T(8,128)(2,1)} %get-tuple-element.39.query, bf16[4096,512]{1,0:T(8,128)(2,1)} %get-tuple-element.40.keys, bf16[4096,512]{1,0:T(8,128)(2,1)} %get-tuple-element.41.vals, bf16[4096,128]{1,0:T(8,128)(2,1)} %maximum_maximum_fusion.key_aug, ...), custom_call_target="tpu_custom_call" | custom-call | tf_op jit(solution)/shard_map/pallas_call | solution.py:642
  76.8 20.0 %shard_map.325 = (bf16[1024,512]{1,0:T(8,128)(2,1)}, bf16[1024,512]{1,0:T(8,128)(2,1)}, bf16[1024,512]{1,0:T(8,128)(2,1)}, bf16[4,1024,128]{2,1,0:T(8,128)(2,1)}, bf16[2,2816,256]{2,1,0:T(8,128)(2,1)}) custom-call(f32[1024,512]{1,0:T(8,128)} %get-tuple-element.38.enc, f32[1024,512]{1,0:T(8,128)} %get-tuple-element.42.att, ...), custom_call_target="tpu_custom_call" | custom-call | tf_op jit(solution)/shard_map/pallas_call | solution.py:642
  96.8 70.2 %shard_map.326 = (bf16[128,4096]{1,0:T(8,128)(2,1)}, bf16[2,512,256]{2,1,0:T(8,128)(2,1)}, bf16[2,2816,256]{2,1,0:T(8,128)(2,1)}) custom-call(bf16[1024,512]{1,0:T(8,128)(2,1)} %get-tuple-element.39.query, bf16[4,1024,128]{2,1,0:T(8,128)(2,1)} %get-tuple-element.45.query_aug, bf16[1024,512]{1,0:T(8,128)(2,1)} %get-tuple-element.46.grad_att, ...), custom_call_target="tpu_custom_call" | custom-call | tf_op jit(solution)/shard_map/pallas_call | solution.py:642
  167.0 1.3 slice_bitcast_fusion.1
  168.3 0.0 copy-start.1
  168.3 1.6 maximum_convert_fusion.1
  169.9 1.0 copy-done.1
  170.9 0.6 fusion.7
  171.5 0.6 pad_maximum_fusion.1
  172.1 0.1 slice_bitcast_fusion.5
  172.2 1.6 maximum_convert_fusion
  173.8 1.1 maximum_convert_fusion.2
  174.9 27.2 %shard_map.327 = (bf16[2,512,256]{2,1,0:T(8,128)(2,1)}, f32[32,4096]{1,0:T(8,128)}) custom-call(bf16[2,512,256]{2,1,0:T(8,128)(2,1)} %get-tuple-element.53.x, bf16[4,32,4096]{2,1,0:T(8,128)(2,1)} %bitcast.96, bf16[32,4096]{1,0:T(8,128)(2,1)} %bitcast.95, bf16[8,4096]{1,0:T(8,128)(2,1)} %get-tuple-element.98.memt, bf16[8,4096]{1,0:T(8,128)(2,1)} %get-tuple-element.97.trt, ...), custom_call_target="tpu_custom_call" | custom-call | tf_op jit(solution)/shard_map/pallas_call | solution.py:642
  202.1 0.8 slice_reduce_fusion
  202.8 0.2 dynamic-update-slice
  203.1 0.2 dynamic-update-slice.1
  203.3 0.2 dynamic-update-slice.2
  203.5 0.2 dynamic-update-slice.3
  203.7 0.2 dynamic-update-slice.4
  203.9 0.2 dynamic-update-slice.5
  204.1 0.8 bitcast_dynamic-update-slice_fusion.5
  204.9 0.8 bitcast_dynamic-update-slice_fusion.4
  205.8 1.0 bitcast_dynamic-update-slice_fusion.3
  206.8 0.8 bitcast_dynamic-update-slice_fusion.2
  207.6 0.8 bitcast_dynamic-update-slice_fusion.1
  208.4 0.8 bitcast_dynamic-update-slice_fusion
  209.3 0.0 copy-done.2
  209.3 2.3 %convolution_add_fusion = f32[512,1536]{1,0:T(8,128)} fusion(bf16[128,512]{1,0:T(8,128)(2,1)S(1)} %copy-done.2, bf16[128,1536]{1,0:T(8,128)(2,1)S(1)} %bitcast_dynamic-update-slice_fusion, f32[1536]{0:T(1024)S(1)} %convert_element_type.53, f32[512]{0:T(512)S(1)} %copy-done.4), kind=kOutput, calls=%fused_computation | convolution fusion | flops 202899456 | bytes 3678208 | tf_op jit(solution)/shard_map/fe,fo->eo/dot_general | solution.py:798
  211.7 0.5 fusion.11
  212.2 0.6 add.36
  212.8 0.6 fusion.9
  213.4 1.3 fusion.10
  214.7 1.5 dynamic-slice_add_fusion
  216.2 0.8 copy.51
  (25 shorter events, 0.1 us)
Async XLA Ops:
  168.3 2.6 %copy-start.1 = (bf16[2,2816,256]{2,1,0:T(8,128)(2,1)S(1)}, bf16[2,2816,256]{2,1,0:T(8,128)(2,1)}, u32[]{:S(2)}) copy-start(bf16[2,2816,256]{2,1,0:T(8,128)(2,1)} %get-tuple-element.58) | copy-start | bytes 8650756
  171.5 40.7 %copy-start.5 = (f32[1,512]{1,0:T(1,128)}, f32[1,512]{1,0:T(1,128)S(1)}, u32[]{:S(2)}) copy-start(f32[1,512]{1,0:T(1,128)S(1)} %get-tuple-element.92) | copy-start | bytes 6148
  173.8 35.5 %copy-start.2 = (bf16[128,512]{1,0:T(8,128)(2,1)S(1)}, bf16[128,512]{1,0:T(8,128)(2,1)}, u32[]{:S(2)}) copy-start(bf16[128,512]{1,0:T(8,128)(2,1)} %get-tuple-element.50.w_enc) | copy-start | bytes 393220
  173.8 35.5 %copy-start.4 = (f32[512]{0:T(512)S(1)}, f32[512]{0:T(512)}, u32[]{:S(2)}) copy-start(f32[512]{0:T(512)} %param.25) | copy-start | bytes 6148
  205.8 5.9 %copy-start = (bf16[512,1536]{1,0:T(8,128)(2,1)S(1)}, bf16[512,1536]{1,0:T(8,128)(2,1)}, u32[]{:S(2)}) copy-start(bf16[512,1536]{1,0:T(8,128)(2,1)} %w_qkv.1) | copy-start | bytes 4718596
  211.7 4.5 %copy-start.3 = (f32[32,4096]{1,0:T(8,128)S(1)}, f32[32,4096]{1,0:T(8,128)}, u32[]{:S(2)}) copy-start(f32[32,4096]{1,0:T(8,128)} %get-tuple-element.56) | copy-start | bytes 1572868

commit v2 on v1

v2 whole, which is shorter than its diff:
```python
import functools
import math

import jax
import jax.numpy as jnp
from jax import lax
from jax.experimental import pallas as pl
from jax.experimental.pallas import tpu as pltpu
from jax.sharding import PartitionSpec as P

HEADS = 4
HD = 128
FEATS = 100
EPS = 1e-5
LOG2E = 1.4426950408889634
BIG = 1e30
SLOTS = 8
SLOTS_AT = (0, 4, 7, 10, 14)
VMEM_BYTES = 63 * 1024 * 1024

BF = jnp.bfloat16
F32 = jnp.float32
MESH = pl.DeviceIdType.MESH


def dot(a, b):
    return lax.dot_general(a, b, (((1,), (0,)), ((), ())), preferred_element_type=F32)


def dot_nt(a, b):
    return lax.dot_general(a, b, (((1,), (1,)), ((), ())), preferred_element_type=F32)


def dot_tn(a, b):
    return lax.dot_general(a, b, (((0,), (0,)), ((), ())), preferred_element_type=F32)


def split3(v):
    high = v.astype(BF)
    rest = v - high.astype(F32)
    mid = rest.astype(BF)
    return high, mid, (rest - mid.astype(F32)).astype(BF)


def dot_split(v, b):
    high, mid, small = split3(v)
    return dot(high, b) + dot(mid, b) + dot(small, b)


def aug_lanes(base, value):
    high, mid, small = (part.astype(F32) for part in split3(value))
    lane = lax.broadcasted_iota(jnp.int32, base.shape, 1)
    out = jnp.where(lane == SLOTS, high, base.astype(F32))
    out = jnp.where(lane == SLOTS + 1, mid, out)
    return jnp.where(lane == SLOTS + 2, small, out).astype(BF)

def bits_below(count):
    return [1 << i for i in range(count.bit_length() - 1)]


def bit_of(index, bit):
    return lax.rem(index // bit, 2)


def flip(index, bit):
    return index + bit * (1 - 2 * bit_of(index, bit))


def greet(peers):
    barrier = pltpu.get_barrier_semaphore()
    for peer in peers:
        pl.semaphore_signal(barrier, inc=1, device_id=peer, device_id_type=MESH)
    pl.semaphore_wait(barrier, len(peers))


def send(src, dst, sems, slot, peer):
    return pltpu.make_async_remote_copy(
        src_ref=src, dst_ref=dst, send_sem=sems[0].at[slot], recv_sem=sems[1].at[slot],
        device_id=peer, device_id_type=MESH,
    )


def gather_steps(feat_count):
    steps, held = [], [()]
    for bit in bits_below(feat_count)[::-1]:
        steps += [(path, bit) for path in held]
        held = held + [path + (bit,) for path in held]
    return steps


class GatherFeat:
    def __init__(self, full, block, piece, sems, first, feat_count):
        self.full, self.block, self.piece = full, block, piece
        self.sems, self.first = sems, first
        self.steps = gather_steps(feat_count)
        self.me = lax.axis_index("feat")
        self.waited = set()

    def copy(self, number, at):
        path, bit = self.steps[number]
        index = self.me
        for done in path:
            index = flip(index, done)
        part = self.full.at[
            pl.ds(pl.multiple_of(index * self.block, self.block), self.block),
            pl.ds(at * self.piece, self.piece),
        ]
        slot = self.first + at * len(self.steps) + number
        return send(part, part, self.sems, slot, {"feat": flip(self.me, bit)})

    def arrived(self, number, at):
        if (number, at) not in self.waited:
            self.waited.add((number, at))
            self.copy(number, at).wait_recv()

    def start(self, at):
        for number, (path, _) in enumerate(self.steps):
            if not path:
                self.copy(number, at).start()

    def forward(self, at):
        for number, (path, _) in enumerate(self.steps):
            if path:
                self.arrived(self.steps.index((path[:-1], path[-1])), at)
                self.copy(number, at).start()

    def finish(self, at):
        for number in range(len(self.steps)):
            self.arrived(number, at)
        for number in range(len(self.steps)):
            self.copy(number, at).wait_send()


def chunked(items, size):
    return [items[i : i + size] for i in range(0, len(items), size)]


class AllReduce:
    def __init__(self, x, out, first_in, later_in, sems, places, parts, group):
        self.x, self.out = x, out
        self.first_in, self.later_in, self.sems = first_in, later_in, sems
        self.place = {axis: lax.axis_index(axis) for axis in places}
        self.core = bit_of(self.place["feat"], 1)
        groups = chunked(reduce_bits(places), group)
        self.depth = len(groups)
        self.parts = []
        self.count = 2
        start = 0
        for number, size in enumerate(parts):
            turn = number * len(groups) // len(parts)
            at, landing, levels = start, start, []
            length = size
            for bits in groups[turn:] + groups[:turn]:
                length = length // 2 ** len(bits)
                member = sum(self.bit(b) << i for i, b in enumerate(bits))
                peers = []
                for subset in range(1, 2 ** len(bits)):
                    theirs = member
                    where = dict(self.place)
                    for i, (axis, bit) in enumerate(bits):
                        if subset >> i & 1:
                            theirs = theirs + (1 - 2 * self.bit((axis, bit))) * 2**i
                            where[axis] = flip(where[axis], bit)
                    peers.append((where, at + theirs * length, landing, self.count))
                    landing += length
                    self.count += 2
                at = at + member * length
                levels.append((peers, at, length))
            self.parts.append(levels)
            start += size

    def bit(self, which):
        return bit_of(self.place[which[0]], which[1])

    def rows(self, at, size):
        return pl.ds(pl.multiple_of(at, 16), size)

    def core_in(self):
        return send(self.x.at[1 - self.core], self.first_in, self.sems, 0, self.peers()[0])

    def core_out(self):
        half = self.out.at[self.core]
        return send(half, half, self.sems, 1, self.peers()[0])

    def down(self, part, level):
        peers, _, size = self.parts[part][level]
        return [
            send(
                self.x.at[self.core, self.rows(at, size)], self.later_in.at[pl.ds(landing, size)],
                self.sems, slot, where,
            )
            for where, at, landing, slot in peers
        ]

    def up(self, part, level):
        peers, at, size = self.parts[part][level]
        seg = self.out.at[self.core, self.rows(at, size)]
        return [send(seg, seg, self.sems, slot + 1, where) for where, _, _, slot in peers]

    def stage(self, number):
        depth = self.depth
        everyone = range(len(self.parts))
        if number == 0:
            self.core_in().start()
        elif number == 1:
            self.core_in().wait()
            total = self.x[self.core].astype(F32) + self.first_in[...].astype(F32)
            self.x[self.core] = total.astype(BF)
            for part in everyone:
                start_all(self.down(part, 0))
        elif number <= depth + 1:
            level = number - 2
            for part in everyone:
                wait_all(self.down(part, level))
                peers, at, size = self.parts[part][level]
                total = self.x[self.core, self.rows(at, size), :].astype(F32)
                for _, _, landing, _ in peers:
                    total = total + self.later_in[landing : landing + size, :].astype(F32)
                if level + 1 < depth:
                    self.x[self.core, self.rows(at, size), :] = total.astype(BF)
                    start_all(self.down(part, level + 1))
                else:
                    self.out[self.core, self.rows(at, size), :] = total.astype(BF)
                    start_all(self.up(part, level))
        elif number <= 2 * depth + 1:
            level = depth - 1 - (number - depth - 2)
            for part in everyone:
                wait_all(self.up(part, level))
                if level > 0:
                    start_all(self.up(part, level - 1))
            if level == 0:
                self.core_out().start()
        else:
            self.core_out().wait()

    @property
    def stages(self):
        return 2 * self.depth + 3

    def peers(self):
        first = dict(self.place)
        first["feat"] = flip(first["feat"], 1)
        return [first] + [where for peers, _, _ in self.parts[0] for where, _, _, _ in peers]


def start_all(copies):
    for copy in copies:
        copy.start()


def wait_all(copies):
    for copy in copies:
        copy.wait()


def reduce_bits(places):
    return [("feat", b) for b in bits_below(places["feat"])[1:]] + [
        ("rows", b) for b in bits_below(places["rows"])
    ]


def reduce_plan(rows_needed, places, group):
    bits = reduce_bits(places)
    groups = chunked(bits, group)
    granule = 16 * 2 ** len(bits)
    units = -(-rows_needed // granule)
    first = -(-units * 2 // 3)
    parts = [first, units - first] if len(groups) > 1 and units > 1 else [units]
    parts = [size * granule for size in parts]
    sems = 2 + 2 * len(parts) * sum(2 ** len(g) - 1 for g in groups)
    landing = sum(parts)
    return sum(parts), parts, sems, landing


def tile_lanes(v, wide):
    return jnp.concatenate([v] * (wide // v.shape[1]), axis=1)


def table_masks(refs, mem_t, tr_t, key_aug, tab):
    lengths, trains, used = refs
    tables = lengths.shape[1]
    slots, rows = mem_t.shape
    row = lax.broadcasted_iota(jnp.int32, (slots, rows), 0)
    at = lax.broadcasted_iota(jnp.int32, (slots, rows), 1)
    lane = lax.broadcasted_iota(jnp.int32, (1, HD), 1)
    slot = lax.broadcasted_iota(jnp.int32, (8, slots), 1)
    line = lax.broadcasted_iota(jnp.int32, (8, slots), 0)
    member = jnp.zeros((slots, rows), jnp.bool_)
    train = jnp.zeros((slots, rows), jnp.bool_)
    low = jnp.full((1, HD), rows, jnp.int32)
    high = jnp.full((1, HD), 0, jnp.int32)
    counts = jnp.where(line < 2, 1, 0)
    start = jnp.int32(0)
    for j in range(tables):
        stop = start + lengths[0, j]
        learned = start + trains[0, j]
        here = (row == j) & (at >= start)
        member = member | (here & (at < stop))
        train = train | (here & (at < learned))
        low = jnp.where(lane == j, start, low)
        high = jnp.where(lane == j, learned, high)
        counts = jnp.where((slot == j) & (line == 0), trains[0, j], counts)
        counts = jnp.where((slot == j) & (line > 0), used[0, j], counts)
        start = stop
    mem_t[...] = jnp.where(member, 1.0, 0.0).astype(BF)
    tr_t[...] = jnp.where(train, 1.0, 0.0).astype(BF)
    counts = counts.astype(F32)
    tab[...] = jnp.where(line[...] == 1, jnp.sqrt(FEATS / jnp.maximum(counts, 1.0)), counts)
    step = 512

    @pl.loop(0, rows // step)
    def _(block):
        token = lax.broadcasted_iota(jnp.int32, (step, HD), 0) + block * step
        wide = lax.broadcasted_iota(jnp.int32, (step, HD), 1)
        open_to = (token >= low) & (token < high)
        mask = jnp.where(wide < SLOTS, jnp.where(open_to, 0.0, -BIG), 0.0)
        ones = (wide >= SLOTS) & (wide < SLOTS + 3)
        key_aug[pl.ds(pl.multiple_of(block * step, step), step), :] = jnp.where(
            ones, 1.0, mask
        ).astype(BF)

    return start


def layer_kernel(
    lengths, trains, used, features_t, w_mine, b_enc, b_query, b_value, b_out, gain_one, shift_one,
    b_up, b_down, gain_two, shift_two,
    w_qkv_h, w_out_h, w_up_h, w_down_h, cot_h,
    out_h, early_h, late_out, grad_x, w_enc,
    w_out, w_up, w_down, cot,
    mem_t, tr_t, tab, key_aug, cent, normed_t, w_pair, keys, vals, query, enc, att,
    query_aug, grad_att, att_aug, sbuf,
    small, attl_s, gbl_s, o1_s, gffn_s, gpre_s, act_s,
    early_x, early_o, first_e, later_e, grad_low,
    late_x, first_l, later_l, held, grad_in,
    local_sem, gsend, grecv, esend, erecv, lsend, lrecv, rsend, rrecv,
    *, places, early_parts, early_group, late_parts, late_group,
):
    feat_count = places["feat"]
    me = lax.axis_index("feat")
    cols_mine, rows = features_t.shape
    columns, width = w_enc.shape
    hidden = w_up.shape[1]
    rows_mine = query.shape[0]
    row_lo = pl.multiple_of(me * rows_mine, rows_mine)
    col_lo = pl.multiple_of(me * cols_mine, cols_mine)
    half = width // 2

    early = AllReduce(
        early_x, early_o, first_e, later_e, (esend, erecv), places, early_parts, early_group
    )
    late = AllReduce(
        late_x, late_out, first_l, later_l, (lsend, lrecv), places, late_parts, late_group
    )
    w_qkv = [ref.at[0:width, :] for ref in (gbl_s, o1_s, gffn_s)]
    loads = [
        pltpu.make_async_copy(src, dst, local_sem.at[i])
        for i, (src, dst) in enumerate(
            [
                (w_qkv_h.at[:, pl.ds(part * width, width)], w_part)
                for part, w_part in enumerate(w_qkv)
            ]
            + [(cot_h, cot), (w_out_h, w_out), (w_up_h, w_up), (w_down_h, w_down)]
        )
    ]
    start_all(loads)
    greet(late.peers())

    w_enc[pl.ds(col_lo, cols_mine), :] = w_mine[...]
    steps = len(gather_steps(feat_count))
    gather_w = GatherFeat(w_enc, cols_mine, width, (gsend, grecv), 0, feat_count)
    gather_w.start(0)

    table_masks((lengths, trains, used), mem_t, tr_t, key_aug, tab)
    step = 512
    pieces = [slice(at, at + step) for at in range(0, rows, step)]
    count = tab[0:1, :]
    mean = jnp.zeros((cols_mine, SLOTS), F32)
    for cut in pieces:
        mean = mean + dot_nt(features_t[:, cut], tr_t[:, cut])
    mean = mean / count
    var = jnp.zeros((cols_mine, SLOTS), F32)
    for cut in pieces:
        c = features_t[:, cut].astype(F32) - dot_split(mean, mem_t[:, cut])
        cent[:, cut] = c
        high, mid, _ = split3(c * c)
        var = var + (dot_nt(high, tr_t[:, cut]) + dot_nt(mid, tr_t[:, cut]))
    var = var / count
    column = (lax.broadcasted_iota(jnp.int32, (cols_mine, SLOTS), 0) + col_lo).astype(F32)
    factor = jnp.where(
        column < tab[2:3, :], lax.rsqrt(jnp.maximum(var, 0.25)) * tab[1:2, :], 0.0
    )
    for cut in pieces:
        normed_t[pl.ds(col_lo, cols_mine), cut] = (
            cent[:, cut] * dot_split(factor, mem_t[:, cut])
        ).astype(BF)
    splits = 4
    piece = rows // splits
    gather_x = GatherFeat(normed_t, cols_mine, piece, (gsend, grecv), steps, feat_count)
    for at in range(splits):
        gather_x.start(at)

    gather_w.forward(0)
    gather_w.finish(0)
    wait_all(loads[:3])
    bias = []
    for part, w_part in enumerate(w_qkv):
        lanes = slice(part * width, (part + 1) * width)
        high, mid, _ = split3(dot(w_enc[...], w_part[...]))
        w_pair[0:columns, lanes] = high
        w_pair[columns:, lanes] = mid
        bias.append(dot_split(jnp.broadcast_to(b_enc[...], (8, width)), w_part[...])[0:1, :])
    bias_q, bias_k, bias_v = bias[0] + b_query[...], bias[1], bias[2] + b_value[...]

    def project(at):
        for lo in range(at * piece, (at + 1) * piece, step):
            n = normed_t[:, lo : lo + step].astype(F32).T.astype(BF)
            both = jnp.concatenate([n, n], axis=1)
            keys[lo : lo + step, :] = (
                dot(both, w_pair[:, width : 2 * width]) + bias_k
            ).astype(BF)
            vals[lo : lo + step, :] = (
                dot(both, w_pair[:, 2 * width :]) + bias_v
            ).astype(BF)

    gather_x.forward(0)
    for at in range(splits):
        if at + 1 < splits:
            gather_x.forward(at + 1)
        gather_x.finish(at)
        project(at)
    block = min(256, rows_mine)
    scale = LOG2E / math.sqrt(HD)
    for lo in range(0, rows_mine, block):
        cols = pl.ds(pl.multiple_of(row_lo + lo, block), block)
        n = normed_t[:, cols].astype(F32).T.astype(BF)
        both = jnp.concatenate([n, n], axis=1)
        query[lo : lo + block, :] = (
            (dot(both, w_pair[:, 0:width]) + bias_q) * scale
        ).astype(BF)
        enc[lo : lo + block, :] = dot(n, w_enc[...]) + b_enc[...]

    q_step = min(256, rows_mine)
    k_step = 512
    ones = jnp.ones((k_step, HD), BF)

    @pl.loop(0, rows_mine // q_step)
    def _(number):
        lo = pl.multiple_of(number * q_step, q_step)
        q_rows = pl.ds(lo, q_step)
        cols = pl.ds(pl.multiple_of(row_lo + lo, q_step), q_step)
        table = jnp.concatenate(
            [mem_t[:, cols].astype(F32), jnp.zeros((HD - SLOTS, q_step), F32)], axis=0
        ).T.astype(BF)
        for head in range(HEADS):
            lanes = slice(head * HD, (head + 1) * HD)
            q = jnp.concatenate([query[q_rows, lanes], table], axis=1)
            peak = jnp.full((q_step, HD), -3e38, F32)
            for at in range(0, rows, k_step):
                k_rows = slice(at, at + k_step)
                k = jnp.concatenate([keys[k_rows, lanes], key_aug[k_rows, :]], axis=1)
                s = dot_nt(q, k)
                sbuf[head % 2, :, k_rows] = s
                for lo in range(0, k_step, HD):
                    peak = jnp.maximum(peak, s[:, lo : lo + HD])
            top = jnp.broadcast_to(jnp.max(peak, axis=1, keepdims=True), (q_step, HD))
            total = jnp.zeros((q_step, 2 * HD), F32)
            for at in range(0, rows, k_step):
                k_rows = slice(at, at + k_step)
                p = jnp.exp2(sbuf[head % 2, :, k_rows] - tile_lanes(top, k_step)).astype(BF)
                v = jnp.concatenate([vals[k_rows, lanes], ones], axis=1)
                total = total + dot(p, v)
            norm = total[:, HD:]
            att[q_rows, lanes] = total[:, :HD] / norm
            query_aug[head, q_rows, :] = aug_lanes(table, -(top + jnp.log2(norm)))

    wait_all(loads[3:])
    small[...] = jnp.zeros(small.shape, F32)

    def add_small(slot, value, wide):
        small[slot : slot + 1, 0:wide] += jnp.sum(value, axis=0, keepdims=True)

    def mean_of(v):
        return jnp.mean(v, axis=1, keepdims=True)

    @pl.loop(0, rows_mine // block)
    def _(number):
        at = pl.ds(pl.multiple_of(number * block, block), block)
        attended = att[at, :]
        attl = attended.astype(BF)
        attl_s[at, :] = attl
        resid = enc[at, :] + dot(attl, w_out[...]) + b_out[...]
        ctr = resid - mean_of(resid)
        rstd1 = lax.rsqrt(mean_of(ctr * ctr) + EPS)
        n1 = ctr * rstd1
        o1 = n1 * gain_one[...] + shift_one[...]
        o1l = o1.astype(BF)
        o1_s[at, :] = o1l
        pre = dot(o1l, w_up[...]) + b_up[...]
        cdf = 0.5 + 0.5 * lax.erf(pre * (1.0 / math.sqrt(2.0)))
        slope = cdf + pre * (jnp.exp(-0.5 * pre * pre) * (1.0 / math.sqrt(2.0 * math.pi)))
        actl = (pre * cdf).astype(BF)
        act_s[at, :] = actl
        r2 = o1 + dot(actl, w_down[...]) + b_down[...]
        ctr2 = r2 - mean_of(r2)
        rstd2 = lax.rsqrt(mean_of(ctr2 * ctr2) + EPS)
        n2 = ctr2 * rstd2
        go = cot[at, :].astype(F32)
        cot[at, :] = (n2 * gain_two[...] + shift_two[...]).astype(BF)
        add_small(0, go * n2, width)
        add_small(1, go, width)
        dn = go * gain_two[...]
        g2 = rstd2 * (dn - mean_of(dn) - n2 * mean_of(dn * n2))
        gfl = g2.astype(BF)
        gffn_s[at, :] = gfl
        add_small(2, g2, width)
        gpl = (dot_nt(gfl, w_down[...]) * slope).astype(BF)
        gpre_s[at, :] = gpl
        add_small(3, gpl.astype(F32), hidden)
        g1 = dot_nt(gpl, w_up[...]) + g2
        add_small(4, g1 * n1, width)
        add_small(5, g1, width)
        dn1 = g1 * gain_one[...]
        gr = rstd1 * (dn1 - mean_of(dn1) - n1 * mean_of(dn1 * n1))
        add_small(6, gr, width)
        gbl = gr.astype(BF)
        gbl_s[at, :] = gbl
        ga = dot_nt(gbl, w_out[...]).astype(BF)
        grad_att[at, :] = ga
        prod = ga.astype(F32) * attended
        zero = jnp.zeros((block, HD), BF)
        for head in range(HEADS):
            lanes = slice(head * HD, (head + 1) * HD)
            row_sum = jnp.sum(prod[:, lanes], axis=1, keepdims=True)
            att_aug[head, at, :] = aug_lanes(zero, jnp.broadcast_to(-row_sum, (block, HD)))

    store_out = pltpu.make_async_copy(cot, out_h, local_sem.at[7])
    store_out.start()

    def pack(at, value):
        into = slice(at, at + value.shape[0])
        early_x[0, into, :] = value[:, :half].astype(BF)
        early_x[1, into, :] = value[:, half:].astype(BF)

    own = pl.ds(row_lo, rows_mine)
    tile = 256
    for at in range(0, width, tile):
        pack(at, dot_tn(attl_s[:, at : at + tile], gbl_s[...]))
    base = width
    for at in range(0, width, tile):
        up = dot_tn(o1_s[:, at : at + tile], gpre_s[...])
        for part in range(hidden // width):
            pack(base + part * width + at, up[:, part * width : (part + 1) * width])
    base = base + hidden
    for at in range(0, hidden, tile):
        pack(base + at, dot_tn(act_s[:, at : at + tile], gffn_s[...]))
    base = base + hidden
    pack(base, dot(normed_t[:, own], gbl_s[...]))
    base = base + columns
    pack(base, jnp.concatenate([small[:, :width], small[:, width:]], axis=0))
    base = base + 16
    if base < early_x.shape[1]:
        early_x[:, base:, :] = jnp.zeros((2, early_x.shape[1] - base, half), BF)
    early.stage(0)

    dq = att
    grad_normed = sbuf.at[0, 0:columns, :]
    moment = sbuf.at[0, columns : 2 * columns, 0 : 3 * width]
    mine = sbuf.at[1, 0:cols_mine, :]
    colsum = sbuf.at[1, cols_mine : cols_mine + 8, 0 : 3 * width]
    dq[...] = jnp.zeros(dq.shape, F32)
    moment[...] = jnp.zeros(moment.shape, F32)
    colsum[...] = jnp.zeros(colsum.shape, F32)
    dkv = act_s
    slots = SLOTS_AT[: min(len(SLOTS_AT), early.stages - 1)]

    @pl.loop(0, rows // k_step)
    def _(chunk):
        k_rows = pl.ds(pl.multiple_of(chunk * k_step, k_step), k_step)
        aug = key_aug[k_rows, :]
        for head in range(HEADS):
            lanes = slice(head * HD, (head + 1) * HD)
            q = query[:, lanes]
            k = keys[k_rows, lanes]
            do = grad_att[:, lanes]
            s = dot_nt(
                jnp.concatenate([k, aug], axis=1),
                jnp.concatenate([q, query_aug[head]], axis=1),
            )
            p = jnp.exp2(s)
            dp = dot_nt(
                jnp.concatenate([vals[k_rows, lanes], aug], axis=1),
                jnp.concatenate([do, att_aug[head]], axis=1),
            )
            ds = (p * dp).astype(BF)
            dv = dot(p.astype(BF), do)
            dk = dot(ds, q) * (1.0 / LOG2E)
            k_lanes = slice(head * HD, (head + 1) * HD)
            v_lanes = slice(width + head * HD, width + (head + 1) * HD)
            dkv[0:k_step, k_lanes] = dk.astype(BF)
            dkv[0:k_step, v_lanes] = dv.astype(BF)
            for part, value in ((1, dk), (2, dv)):
                lo = part * width + head * HD
                colsum[0:1, lo : lo + HD] += jnp.sum(value, axis=0, keepdims=True)
            dq[:, lanes] += dot_tn(ds, k)
            if head % 2 == 1:
                for number, when in enumerate(slots):

                    @pl.when(2 * chunk + head // 2 == when)
                    def _(number=number):
                        early.stage(number + 1)

        grads = dkv[0:k_step, :]
        moment[:, width:] += dot(normed_t[:, k_rows], grads)
        grad_normed[:, k_rows] = dot_nt(w_pair[0:columns, width:], grads)

    dql = (dq[...] * (1.0 / math.sqrt(HD))).astype(BF)
    colsum[0:1, 0:width] = jnp.sum(dql.astype(F32), axis=0, keepdims=True)
    moment[:, 0:width] = dot(normed_t[:, own], dql)
    grad_normed[:, own] += dot_nt(w_pair[0:columns, 0:width], dql) + dot_nt(w_enc[...], gbl_s[...])
    for i in range(feat_count):
        grad_low[i] = grad_normed[i * cols_mine : (i + 1) * cols_mine, :].astype(BF)

    order = bits_below(feat_count)
    index, number = {}, 0
    for bit in order:
        for i in range(feat_count // (2 * bit)):
            index[bit, i] = number
            number += 1

    def copy(bit, i):
        j = 1 - bit_of(me, bit) + 2 * i
        src = grad_low.at[j] if bit == 1 else held.at[index[bit // 2, 0] + j]
        return send(
            src, grad_in.at[index[bit, i]], (rsend, rrecv), index[bit, i],
            {"feat": flip(me, bit)},
        )

    start_all([copy(1, i) for i in range(feat_count // 2)])
    late_x[...] = jnp.zeros(late_x.shape, BF)
    for part in range(3):
        for side in range(2):
            lanes = slice(part * width + side * half, part * width + (side + 1) * half)
            late_x[side, part * columns : (part + 1) * columns, :] = moment[:, lanes].astype(BF)
            at = 3 * columns + 16 * part
            late_x[side, at : at + 16, :] = jnp.concatenate(
                [colsum[:, lanes], jnp.zeros((8, half), F32)], axis=0
            ).astype(BF)
    late.stage(0)
    for level, bit in enumerate(order):
        for i in range(feat_count // (2 * bit)):
            copy(bit, i).wait()
            j = bit_of(me, bit) + 2 * i
            here = grad_low[j] if bit == 1 else held[index[bit // 2, 0] + j]
            total = here.astype(F32) + grad_in[index[bit, i]].astype(F32)
            if level + 1 < len(order):
                held[index[bit, i]] = total.astype(BF)
            else:
                mine[...] = total
        if level + 1 < len(order):
            start_all([copy(2 * bit, i) for i in range(feat_count // (4 * bit))])
        if level == 0:
            late.stage(1)
    for number in range(len(slots) + 1, early.stages):
        early.stage(number)
    store_early = pltpu.make_async_copy(early_o, early_h, local_sem.at[8])
    store_early.start()

    def gather(v, member):
        high, mid, small = split3(v)
        return dot_nt(high, member) + dot_nt(mid, member) + dot_nt(small, member)

    d_factor = jnp.zeros((cols_mine, SLOTS), F32)
    for cut in pieces:
        d_factor = d_factor + gather(mine[:, cut] * cent[:, cut], mem_t[:, cut])
    late.stage(2)
    side = jnp.where(var > 0.25, 1.0, jnp.where(var == 0.25, 0.5, 0.0))
    d_var = d_factor * (-0.5) * factor / jnp.maximum(var, 0.25) * side
    pull = 2.0 * d_var / count
    d_mean = jnp.zeros((cols_mine, SLOTS), F32)
    for cut in pieces:
        dc = mine[:, cut] * dot_split(factor, mem_t[:, cut]) + cent[:, cut] * dot_split(
            pull, tr_t[:, cut]
        )
        grad_x[:, cut] = dc
        d_mean = d_mean - gather(dc, mem_t[:, cut])
    d_mean = d_mean / count
    for cut in pieces:
        grad_x[:, cut] = grad_x[:, cut] + dot_split(d_mean, tr_t[:, cut])
    for number in range(3, late.stages):
        late.stage(number)
    store_out.wait()
    store_early.wait()


def finish_kernel(
    early, late, w_enc, w_qkv, b_enc,
    g_w_enc, g_b_enc, g_w_qkv, g_b_query, g_b_value, g_w_out, g_b_out, g_gain_one,
    g_shift_one, g_w_up, g_b_up, g_w_down, g_b_down, g_gain_two, g_shift_two,
    moment_s, sums_s, *, places,
):
    columns, width = w_enc.shape
    hidden = g_w_up.shape[1]
    half = width // 2
    cols_mine = g_w_enc.shape[0]

    def take(ref, lo, count):
        return jnp.concatenate([ref[0, lo : lo + count, :], ref[1, lo : lo + count, :]], axis=1)

    step = 256
    for lo in range(0, width, step):
        g_w_out[lo : lo + step, :] = take(early, lo, step).astype(F32)
    base = width
    for part in range(hidden // width):
        for lo in range(0, width, step):
            g_w_up[lo : lo + step, part * width : (part + 1) * width] = take(
                early, base + part * width + lo, step
            ).astype(F32)
    base = base + hidden
    for lo in range(0, hidden, step):
        g_w_down[lo : lo + step, :] = take(early, base + lo, step).astype(F32)
    base = base + hidden
    for part in range(3):
        moment_s[:, part * width : (part + 1) * width] = take(late, part * columns, columns)
        sums_s[:, part * width : (part + 1) * width] = take(
            late, 3 * columns + 16 * part, 16
        )
    sums = sums_s[0:1, :].astype(F32)
    b_high, b_mid, b_low = split3(b_enc[...])
    for lo in range(0, 3 * width, width):
        cut = slice(lo, lo + width)
        s = sums_s[0:1, cut]
        outer = dot_tn(b_high, s) + dot_tn(b_mid, s) + dot_tn(b_low, s)
        g_w_qkv[:, cut] = dot_tn(w_enc[...], moment_s[:, cut]) + outer
    me = lax.axis_index("feat")
    own = pl.ds(pl.multiple_of(me * cols_mine, cols_mine), cols_mine)
    own_local = pl.ds(pl.multiple_of(base + me * cols_mine, cols_mine), cols_mine)
    local = jnp.concatenate([early[0, own_local, :], early[1, own_local, :]], axis=1)
    g_w_enc[...] = dot_nt(moment_s[own, :], w_qkv[...]) + local.astype(F32)
    small = take(early, base + columns, 16).astype(F32)
    g_b_enc[...] = dot_nt(sums_s[...], w_qkv[...])[0:1, :] + small[6:7, :]
    g_b_query[...] = sums[:, :width]
    g_b_value[...] = sums[:, 2 * width :]
    g_b_out[...] = small[6:7, :]
    g_gain_one[...] = small[4:5, :]
    g_shift_one[...] = small[5:6, :]
    g_b_up[...] = jnp.concatenate([small[3:4, :], small[11:12, :]], axis=1)
    g_b_down[...] = small[2:3, :]
    g_gain_two[...] = small[0:1, :]
    g_shift_two[...] = small[1:2, :]


def spec(kind):
    return pl.BlockSpec(memory_space={"v": pltpu.VMEM, "s": pltpu.SMEM, "h": pl.ANY}[kind])


def call(kernel, ins, args, outs, scratch, **params):
    return pl.pallas_call(
        kernel,
        out_shape=tuple(jax.ShapeDtypeStruct(shape, kind) for _, shape, kind in outs),
        in_specs=[spec(k) for k in ins],
        out_specs=tuple(spec(k) for k, _, _ in outs),
        scratch_shapes=[
            pltpu.SemaphoreType.DMA((entry,)) if isinstance(entry, int) else pltpu.VMEM(*entry)
            for entry in scratch
        ],
        compiler_params=pltpu.CompilerParams(vmem_limit_bytes=VMEM_BYTES, **params),
    )(*args)


def per_device(
    features, lengths, train_counts, used_features, w_enc, b_enc, w_qkv, b_query, b_value,
    w_out, b_out, gain_one, shift_one, w_up, b_up, w_down, b_down, gain_two, shift_two, cotangent,
):
    places = {"feat": lax.axis_size("feat"), "rows": lax.axis_size("rows")}
    feat_count = places["feat"]
    rows, cols_mine = features.shape
    columns = cols_mine * feat_count
    width = w_qkv.shape[0]
    hidden = w_up.shape[1]
    rows_mine = rows // feat_count
    half = width // 2
    early_group, late_group = 2, 4
    early_rows, early_parts, early_sems, early_land = reduce_plan(
        width + 2 * hidden + columns + 16, places, early_group
    )
    late_rows, late_parts, late_sems, late_land = reduce_plan(
        3 * columns + 48, places, late_group
    )
    row = lambda v: v.reshape(1, -1)
    gather_sems = 5 * (feat_count - 1)
    out, early, late, grad_x, w_enc_all = call(
        functools.partial(
            layer_kernel, places=places, early_parts=early_parts, early_group=early_group,
            late_parts=late_parts, late_group=late_group,
        ),
        "sss" + "v" * 12 + "h" * 5,
        (
            lengths, train_counts, used_features, features.T, w_enc, row(b_enc), row(b_query),
            row(b_value), row(b_out), row(gain_one), row(shift_one), row(b_up), row(b_down),
            row(gain_two), row(shift_two), w_qkv, w_out, w_up, w_down, cotangent,
        ),
        [
            ("h", (rows_mine, width), BF), ("h", (2, early_rows, half), BF),
            ("v", (2, late_rows, half), BF), ("v", (cols_mine, rows), F32),
            ("v", (columns, width), BF),
        ],
        [
            (w_out.shape, BF), (w_up.shape, BF), (w_down.shape, BF),
            ((rows_mine, width), BF),
            ((SLOTS, rows), BF), ((SLOTS, rows), BF), ((8, SLOTS), F32), ((rows, HD), BF),
            ((cols_mine, rows), F32), ((columns, rows), BF), ((2 * columns, 3 * width), BF),
            ((rows, width), BF), ((rows, width), BF), ((rows_mine, width), BF),
            ((rows_mine, width), F32), ((rows_mine, width), F32),
            ((HEADS, rows_mine, HD), BF), ((rows_mine, width), BF), ((HEADS, rows_mine, HD), BF),
            ((2, min(256, rows_mine), rows), F32),
            ((8, hidden), F32), ((rows_mine, width), BF), ((rows_mine, width), BF),
            ((rows_mine, width), BF), ((rows_mine, width), BF), ((rows_mine, hidden), BF),
            ((rows_mine, hidden), BF),
            ((2, early_rows, half), BF), ((2, early_rows, half), BF), ((early_rows, half), BF),
            ((early_land, half), BF), ((feat_count, cols_mine, rows), BF),
            ((2, late_rows, half), BF), ((late_rows, half), BF), ((late_land, half), BF),
            ((feat_count - 1, cols_mine, rows), BF), ((feat_count - 1, cols_mine, rows), BF),
            9, gather_sems, gather_sems, early_sems, early_sems, late_sems, late_sems,
            feat_count - 1, feat_count - 1,
        ],
        collective_id=0, has_side_effects=True,
    )
    vector = ("v", (1, width), F32)
    grads = call(
        functools.partial(finish_kernel, places=places),
        "v" * 5,
        (early, late, w_enc_all, w_qkv, row(b_enc)),
        [
            ("v", (cols_mine, width), F32), vector,
            ("v", (width, 3 * width), F32), vector, vector, ("v", (width, width), F32), vector,
            vector, vector, ("v", (width, hidden), F32), ("v", (1, hidden), F32),
            ("v", (hidden, width), F32), vector, vector, vector,
        ],
        [((columns, 3 * width), BF), ((16, 3 * width), BF)],
    )
    return (out, grad_x.T) + tuple(g.reshape(-1) if g.shape[0] == 1 else g for g in grads)


def solution(mesh):
    whole = P()
    in_specs = (
        (P("rows", "feat"),) + (P("rows", None),) * 3 + (P("feat", None),) + (whole,) * 14
        + (P(("rows", "feat"), None),)
    )
    out_specs = (
        (P(("rows", "feat"), None), P("rows", "feat"), P("feat", None)) + (whole,) * 14
    )
    return jax.shard_map(
        per_device, mesh=mesh, in_specs=in_specs, out_specs=out_specs, check_vma=False
    )
```

time: 218 us -> 151 us (0.69)
  Pallas kernels: 186 us -> 147 us
  other arithmetic: 13.1 us -> 0 us
  local copies, waits for them, and re-layouts: 13.4 us -> 3.12 us
  matrix products: 4.1 us -> 0 us
    pallas_call x5 -> x2, Pallas kernels: 186 us -> 147 us  [call(): pl.pallas_call(kernel, out_shape=tuple((jax.ShapeDtypeStruct(shape, kind)...]
    convert_element_type x8 -> x0, other arithmetic: 6.2 us -> none  [the longest x1 1.61 us: per_device(): grad_w_down = take(early, base, hidden).astype(F32)]
    unnamed x24 -> x4, local copies, waits for them, and re-layouts: 7.33 us -> 3.12 us
    dot_general x3 -> x0, matrix products: 4.1 us -> none  [the longest x1 2.27 us: per_device(): jnp.einsum('fe,fo->eo', w_enc_all, moment, preferred_element_type=F32)]
    add x3 -> x0, other arithmetic: 2.76 us -> none  [the longest x1 1.48 us: per_device(): jnp.einsum('fo,eo->fe', moment, w_qkv, preferred_element_type=F32) + local]
where the time goes in v2:
time: 151 us
  Pallas kernels  147 us (97%)
  local copies, waits for them, and re-layouts  3.12 us (2%)
    pallas_call x2, Pallas kernels, call(): pl.pallas_call(kernel, out_shape=tuple((jax.ShapeDtypeStruct(shape, kind)...  147 us
    unnamed x4, local copies, waits for them, and re-layouts  3.12 us

profile of v2, /device:TPU:0, one launch (start us, length us, event | category | flops | bytes accessed | tf_op | source)
XLA Modules:
  0.0 151.1 jit_solution(17302214853449321579)
XLA Ops:
  0.7 138.8 %shard_map.323 = (bf16[1024,512]{1,0:T(8,128)(2,1)}, bf16[2,2816,256]{2,1,0:T(8,128)(2,1)}, bf16[2,512,256]{2,1,0:T(8,128)(2,1)}, f32[32,4096]{1,0:T(8,128)}, bf16[128,512]{1,0:T(8,128)(2,1)}) custom-call(s32[1,6]{1,0:T(1,128)} %lengths.1, s32[1,6]{1,0:T(1,128)} %trains.1, s32[1,6]{1,0:T(1,128)} %used.1, bf16[32,4096]{1,0:T(8,128)(2,1)} %bitcast.23, ...), custom_call_target="tpu_custom_call" | custom-call | tf_op jit(solution)/shard_map/pallas_call | solution.py:758
  139.5 8.5 %shard_map.324 = (f32[32,512]{1,0:T(8,128)}, f32[1,512]{1,0:T(1,128)}, f32[512,1536]{1,0:T(8,128)}, f32[1,512]{1,0:T(1,128)}, f32[1,512]{1,0:T(1,128)}, /*index=...) custom-call(bf16[2,2816,256]{2,1,0:T(8,128)(2,1)} %get-tuple-element, ...), custom_call_target="tpu_custom_call" | custom-call | tf_op jit(solution)/shard_map/pallas_call | solution.py:758
  148.0 0.0 copy-start
  148.0 2.3 %copy.39 = bf16[1024,512]{1,0:T(8,128)(2,1)} copy(bf16[1024,512]{1,0:T(8,128)(2,1)} %get-tuple-element.74) | data formatting | bytes 2097152
  150.3 0.0 copy-done
  150.3 0.8 copy.40
Async XLA Ops:
  148.0 2.3 %copy-start = (f32[32,4096]{1,0:T(8,128)S(1)}, f32[32,4096]{1,0:T(8,128)}, u32[]{:S(2)}) copy-start(f32[32,4096]{1,0:T(8,128)} %get-tuple-element.38) | copy-start | bytes 1572868

commit v3 on v2

v3 whole, which is shorter than its diff:
```python
import functools
import math

import jax
import jax.numpy as jnp
from jax import lax
from jax.experimental import pallas as pl
from jax.experimental.pallas import tpu as pltpu
from jax.sharding import PartitionSpec as P

HEADS = 4
HD = 128
FEATS = 100
EPS = 1e-5
LOG2E = 1.4426950408889634
BIG = 1e30
SLOTS = 8
PASSES = 2
EARLY_AT = (0, 4, 7, 10)
LATE_AT = (1, 6)
VMEM_BYTES = 63 * 1024 * 1024

BF = jnp.bfloat16
F32 = jnp.float32
MESH = pl.DeviceIdType.MESH


def dot(a, b):
    return lax.dot_general(a, b, (((1,), (0,)), ((), ())), preferred_element_type=F32)


def dot_nt(a, b):
    return lax.dot_general(a, b, (((1,), (1,)), ((), ())), preferred_element_type=F32)


def dot_tn(a, b):
    return lax.dot_general(a, b, (((0,), (0,)), ((), ())), preferred_element_type=F32)


def split3(v):
    high = v.astype(BF)
    rest = v - high.astype(F32)
    mid = rest.astype(BF)
    return high, mid, (rest - mid.astype(F32)).astype(BF)


def dot_split(v, b):
    high, mid, small = split3(v)
    return dot(high, b) + dot(mid, b) + dot(small, b)


def aug_lanes(base, value):
    high, mid, small = (part.astype(F32) for part in split3(value))
    lane = lax.broadcasted_iota(jnp.int32, base.shape, 1)
    out = jnp.where(lane == SLOTS, high, base.astype(F32))
    out = jnp.where(lane == SLOTS + 1, mid, out)
    return jnp.where(lane == SLOTS + 2, small, out).astype(BF)

def bits_below(count):
    return [1 << i for i in range(count.bit_length() - 1)]


def bit_of(index, bit):
    return lax.rem(index // bit, 2)


def flip(index, bit):
    return index + bit * (1 - 2 * bit_of(index, bit))


def greet(peers):
    barrier = pltpu.get_barrier_semaphore()
    for peer in peers:
        pl.semaphore_signal(barrier, inc=1, device_id=peer, device_id_type=MESH)


def await_greetings(peers):
    pl.semaphore_wait(pltpu.get_barrier_semaphore(), len(peers))


def send(src, dst, sems, slot, peer):
    return pltpu.make_async_remote_copy(
        src_ref=src, dst_ref=dst, send_sem=sems[0].at[slot], recv_sem=sems[1].at[slot],
        device_id=peer, device_id_type=MESH,
    )


def gather_steps(feat_count):
    steps, held = [], [()]
    for bit in bits_below(feat_count)[::-1]:
        steps += [(path, bit) for path in held]
        held = held + [path + (bit,) for path in held]
    return steps


def feat_others(me, feat_count):
    bits = bits_below(feat_count)
    subsets = sorted(range(1, feat_count), key=lambda subset: bin(subset).count("1"))
    found = []
    for subset in subsets:
        at = me
        for bit in bits:
            if subset & bit:
                at = flip(at, bit)
        found.append(at)
    return found


class GatherFeat:
    def __init__(self, full, block, piece, sems, first, feat_count):
        self.full, self.block, self.piece = full, block, piece
        self.sems, self.first = sems, first
        self.steps = gather_steps(feat_count)
        self.me = lax.axis_index("feat")
        self.waited = set()

    def copy(self, number, at):
        path, bit = self.steps[number]
        index = self.me
        for done in path:
            index = flip(index, done)
        part = self.full.at[
            pl.ds(pl.multiple_of(index * self.block, self.block), self.block),
            pl.ds(at * self.piece, self.piece),
        ]
        slot = self.first + at * len(self.steps) + number
        return send(part, part, self.sems, slot, {"feat": flip(self.me, bit)})

    def arrived(self, number, at):
        if (number, at) not in self.waited:
            self.waited.add((number, at))
            self.copy(number, at).wait_recv()

    def start(self, at):
        for number, (path, _) in enumerate(self.steps):
            if not path:
                self.copy(number, at).start()

    def forward(self, at):
        for number, (path, _) in enumerate(self.steps):
            if path:
                self.arrived(self.steps.index((path[:-1], path[-1])), at)
                self.copy(number, at).start()

    def finish(self, at):
        for number in range(len(self.steps)):
            self.arrived(number, at)
        for number in range(len(self.steps)):
            self.copy(number, at).wait_send()


def chunked(items, size):
    return [items[i : i + size] for i in range(0, len(items), size)]


class AllReduce:
    def __init__(self, x, out, first_in, later_in, sems, places, parts, group, sem=0):
        self.x, self.out, self.sem, self.size = x, out, sem, sum(parts)
        self.first_in, self.later_in, self.sems = first_in, later_in, sems
        self.place = {axis: lax.axis_index(axis) for axis in places}
        self.core = bit_of(self.place["feat"], 1)
        groups = chunked(reduce_bits(places), group)
        self.depth = len(groups)
        self.parts = []
        self.count = sem + 2
        start = 0
        for number, size in enumerate(parts):
            turn = number * len(groups) // len(parts)
            at, landing, levels = start, start, []
            length = size
            for bits in groups[turn:] + groups[:turn]:
                length = length // 2 ** len(bits)
                member = sum(self.bit(b) << i for i, b in enumerate(bits))
                peers = []
                for subset in range(1, 2 ** len(bits)):
                    theirs = member
                    where = dict(self.place)
                    for i, (axis, bit) in enumerate(bits):
                        if subset >> i & 1:
                            theirs = theirs + (1 - 2 * self.bit((axis, bit))) * 2**i
                            where[axis] = flip(where[axis], bit)
                    peers.append((where, at + theirs * length, landing, self.count))
                    landing += length
                    self.count += 2
                at = at + member * length
                levels.append((peers, at, length))
            self.parts.append(levels)
            start += size

    def bit(self, which):
        return bit_of(self.place[which[0]], which[1])

    def rows(self, which, side, at, size):
        ref, base = which
        return ref.at[pl.ds(pl.multiple_of(base + side * self.size + at, 16), size)]

    def core_in(self):
        return send(
            self.rows(self.x, 1 - self.core, 0, self.size), self.first_in, self.sems, self.sem,
            self.peers()[0],
        )

    def core_out(self):
        half = self.rows(self.out, self.core, 0, self.size)
        return send(half, half, self.sems, self.sem + 1, self.peers()[0])

    def down(self, part, level):
        peers, _, size = self.parts[part][level]
        return [
            send(
                self.rows(self.x, self.core, at, size), self.later_in.at[pl.ds(landing, size)],
                self.sems, slot, where,
            )
            for where, at, landing, slot in peers
        ]

    def up(self, part, level):
        peers, at, size = self.parts[part][level]
        seg = self.rows(self.out, self.core, at, size)
        return [send(seg, seg, self.sems, slot + 1, where) for where, _, _, slot in peers]

    def stage(self, number):
        depth = self.depth
        everyone = range(len(self.parts))
        if number == 0:
            self.core_in().start()
        elif number == 1:
            self.core_in().wait()
            mine = self.rows(self.x, self.core, 0, self.size)
            mine[...] = (mine[...].astype(F32) + self.first_in[...].astype(F32)).astype(BF)
            for part in everyone:
                start_all(self.down(part, 0))
        elif number <= depth + 1:
            level = number - 2
            for part in everyone:
                wait_all(self.down(part, level))
                peers, at, size = self.parts[part][level]
                mine = self.rows(self.x, self.core, at, size)
                total = mine[...].astype(F32)
                for _, _, landing, _ in peers:
                    total = total + self.later_in[landing : landing + size, :].astype(F32)
                if level + 1 < depth:
                    mine[...] = total.astype(BF)
                    start_all(self.down(part, level + 1))
                else:
                    self.rows(self.out, self.core, at, size)[...] = total.astype(BF)
                    start_all(self.up(part, level))
        elif number <= 2 * depth + 1:
            level = depth - 1 - (number - depth - 2)
            for part in everyone:
                wait_all(self.up(part, level))
                if level > 0:
                    start_all(self.up(part, level - 1))
            if level == 0:
                self.core_out().start()
        else:
            self.core_out().wait()

    @property
    def stages(self):
        return 2 * self.depth + 3

    def peers(self):
        first = dict(self.place)
        first["feat"] = flip(first["feat"], 1)
        return [first] + [where for peers, _, _ in self.parts[0] for where, _, _, _ in peers]


def start_all(copies):
    for copy in copies:
        copy.start()


def wait_all(copies):
    for copy in copies:
        copy.wait()


def reduce_bits(places):
    return [("feat", b) for b in bits_below(places["feat"])[1:]] + [
        ("rows", b) for b in bits_below(places["rows"])
    ]


def reduce_plan(rows_needed, places, group):
    bits = reduce_bits(places)
    groups = chunked(bits, group)
    granule = 16 * 2 ** len(bits)
    units = -(-rows_needed // granule)
    first = -(-units * 2 // 3)
    parts = [first, units - first] if len(groups) > 1 and units > 1 else [units]
    parts = [size * granule for size in parts]
    sems = 2 + 2 * len(parts) * sum(2 ** len(g) - 1 for g in groups)
    landing = sum(parts)
    return sum(parts), parts, sems, landing


def tile_lanes(v, wide):
    return jnp.concatenate([v] * (wide // v.shape[1]), axis=1)


def table_masks(refs, mem_t, tr_t, tab):
    lengths, trains, used = refs
    tables = lengths.shape[1]
    slots, rows = mem_t.shape
    row = lax.broadcasted_iota(jnp.int32, (slots, rows), 0)
    at = lax.broadcasted_iota(jnp.int32, (slots, rows), 1)
    slot = lax.broadcasted_iota(jnp.int32, (8, slots), 1)
    line = lax.broadcasted_iota(jnp.int32, (8, slots), 0)
    member = jnp.zeros((slots, rows), jnp.bool_)
    train = jnp.zeros((slots, rows), jnp.bool_)
    counts = jnp.where(line < 2, 1, 0)
    start = jnp.int32(0)
    for j in range(tables):
        stop = start + lengths[0, j]
        learned = start + trains[0, j]
        here = (row == j) & (at >= start)
        member = member | (here & (at < stop))
        train = train | (here & (at < learned))
        counts = jnp.where((slot == j) & (line == 0), trains[0, j], counts)
        counts = jnp.where((slot == j) & (line > 0), used[0, j], counts)
        start = stop
    mem_t[...] = jnp.where(member, 1.0, 0.0).astype(BF)
    tr_t[...] = jnp.where(train, 1.0, 0.0).astype(BF)
    counts = counts.astype(F32)
    tab[...] = jnp.where(line == 1, jnp.sqrt(FEATS / jnp.maximum(counts, 1.0)), counts)


def key_masks(refs, key_aug):
    lengths, trains = refs
    lane = lax.broadcasted_iota(jnp.int32, (1, HD), 1)
    rows = key_aug.shape[0]
    low = jnp.full((1, HD), rows, jnp.int32)
    high = jnp.full((1, HD), 0, jnp.int32)
    start = jnp.int32(0)
    for j in range(lengths.shape[1]):
        low = jnp.where(lane == j, start, low)
        high = jnp.where(lane == j, start + trains[0, j], high)
        start = start + lengths[0, j]
    step = 512

    @pl.loop(0, rows // step)
    def _(block):
        token = lax.broadcasted_iota(jnp.int32, (step, HD), 0) + block * step
        wide = lax.broadcasted_iota(jnp.int32, (step, HD), 1)
        open_to = (token >= low) & (token < high)
        mask = jnp.where(wide < SLOTS, jnp.where(open_to, 0.0, -BIG), 0.0)
        ones = (wide >= SLOTS) & (wide < SLOTS + 3)
        key_aug[pl.ds(pl.multiple_of(block * step, step), step), :] = jnp.where(
            ones, 1.0, mask
        ).astype(BF)


def layer_kernel(
    lengths, trains, used, features_t, w_mine, b_enc, b_query, b_value, b_out, gain_one, shift_one,
    b_up, b_down, gain_two, shift_two,
    w_qkv_h, w_out_h, w_up_h, w_down_h, cot_h,
    out_h, early_h, late_h, grad_x, w_enc,
    w_out, w_up, w_down, cot,
    mem_t, tr_t, tab, key_aug, cent, normed_t, w_pair, keys, vals, query, enc, att,
    query_aug, grad_att, att_aug, sbuf,
    small, stash, early_x, first_e, later_e, grad_low,
    first_l, later_l, held, grad_in, own_low, own_in,
    local_sem, gsend, grecv, esend, erecv, lsend, lrecv, rsend, rrecv, osend, orecv,
    *, places, early_parts, early_group, late_parts, late_group,
):
    feat_count = places["feat"]
    me = lax.axis_index("feat")
    cols_mine, rows = features_t.shape
    columns, width = w_enc.shape
    hidden = w_up.shape[1]
    rows_mine = query.shape[0]
    row_lo = pl.multiple_of(me * rows_mine, rows_mine)
    col_lo = pl.multiple_of(me * cols_mine, cols_mine)
    half = width // 2

    taken = [0]

    def blocks(count):
        taken[0] += count
        return [
            stash.at[pl.ds(i * rows_mine, rows_mine)] for i in range(taken[0] - count, taken[0])
        ]

    wide_blocks, deep_blocks = width // half, hidden // half
    attl_s, gbl_s, o1_s, gffn_s = (blocks(wide_blocks) for _ in range(4))
    gpre_s, act_s = (blocks(deep_blocks) for _ in range(2))

    def fill(parts, at, value):
        for i, part in enumerate(parts):
            part[at, :] = value[:, i * half : (i + 1) * half]

    def read(parts):
        return jnp.concatenate([part[...] for part in parts], axis=1)

    early_size, late_size = sum(early_parts), sum(late_parts)
    late_x = [2 * early_size + turn * 4 * late_size for turn in range(PASSES)]
    late_o = [at + 2 * late_size for at in late_x]
    early = AllReduce(
        (early_x, 0), (stash, 0), first_e, later_e, (esend, erecv), places, early_parts, early_group
    )
    late_sems = lsend.shape[0] // PASSES
    lates = [
        AllReduce(
            (stash, late_x[turn]), (stash, late_o[turn]), first_l.at[turn], later_l.at[turn],
            (lsend, lrecv), places, late_parts, late_group, turn * late_sems,
        )
        for turn in range(PASSES)
    ]
    w_qkv = [
        [
            stash.at[pl.ds((part * wide_blocks + i) * width, width)]
            for i in range(wide_blocks)
        ]
        for part in range(3)
    ]
    loads = [
        pltpu.make_async_copy(src, dst, local_sem.at[i])
        for i, (src, dst) in enumerate(
            [
                (w_qkv_h.at[:, pl.ds(part * width + i * half, half)], block)
                for part, w_part in enumerate(w_qkv)
                for i, block in enumerate(w_part)
            ]
            + [(cot_h, cot), (w_out_h, w_out), (w_up_h, w_up), (w_down_h, w_down)]
        )
    ]
    start_all(loads)
    peers = lates[0].peers() + [{"feat": at} for at in feat_others(me, feat_count)[2:]]
    greet(peers)

    table_masks((lengths, trains, used), mem_t, tr_t, tab)
    step = 512
    pieces = [slice(at, at + step) for at in range(0, rows, step)]
    count = tab[0:1, :]
    mean = jnp.zeros((cols_mine, SLOTS), F32)
    for cut in pieces:
        mean = mean + dot_nt(features_t[:, cut], tr_t[:, cut])
    mean = mean / count
    var = jnp.zeros((cols_mine, SLOTS), F32)
    for cut in pieces:
        c = features_t[:, cut].astype(F32) - dot_split(mean, mem_t[:, cut])
        cent[:, cut] = c
        high, mid, _ = split3(c * c)
        var = var + (dot_nt(high, tr_t[:, cut]) + dot_nt(mid, tr_t[:, cut]))
    var = var / count
    column = (lax.broadcasted_iota(jnp.int32, (cols_mine, SLOTS), 0) + col_lo).astype(F32)
    is_last = (
        lax.broadcasted_iota(jnp.int32, (cols_mine, 1), 0) + col_lo == columns - 1
    )
    factor = jnp.where(
        column < tab[2:3, :], lax.rsqrt(jnp.maximum(var, 0.25)) * tab[1:2, :], 0.0
    )
    for cut in pieces:
        normed_t[pl.ds(col_lo, cols_mine), cut] = jnp.where(
            is_last, 1.0, cent[:, cut] * dot_split(factor, mem_t[:, cut])
        ).astype(BF)
    w_enc[pl.ds(col_lo, cols_mine), :] = w_mine[...]
    await_greetings(peers)
    steps = len(gather_steps(feat_count))
    gather_w = GatherFeat(w_enc, cols_mine, width, (gsend, grecv), 0, feat_count)
    gather_w.start(0)
    splits = 4
    piece = rows // splits
    gather_x = GatherFeat(normed_t, cols_mine, piece, (gsend, grecv), steps, feat_count)
    for at in range(splits):
        gather_x.start(at)

    key_masks((lengths, trains), key_aug)
    gather_w.forward(0)
    gather_w.finish(0)
    last = lax.broadcasted_iota(jnp.int32, (columns, 1), 0) == columns - 1
    w_enc[...] = jnp.where(last, 0.0, w_enc[...].astype(F32)).astype(BF)
    wait_all(loads[: 3 * wide_blocks])
    for part, w_part in enumerate(w_qkv):
        lanes = slice(part * width, (part + 1) * width)
        w_now = read(w_part)
        bias = dot_split(jnp.broadcast_to(b_enc[...], (8, width)), w_now)[0:1, :]
        if part != 1:
            bias = bias + (b_query if part == 0 else b_value)[...]
        high, mid, _ = split3(jnp.where(last, bias, dot(w_enc[...], w_now)))
        w_pair[0:columns, lanes] = high
        w_pair[columns:, lanes] = mid

    def project(at):
        for lo in range(at * piece, (at + 1) * piece, step):
            n = normed_t[:, lo : lo + step].astype(F32).T.astype(BF)
            both = jnp.concatenate([n, n], axis=1)
            keys[lo : lo + step, :] = dot(both, w_pair[:, width : 2 * width]).astype(BF)
            vals[lo : lo + step, :] = dot(both, w_pair[:, 2 * width :]).astype(BF)

    gather_x.forward(0)
    for at in range(splits):
        if at + 1 < splits:
            gather_x.forward(at + 1)
        gather_x.finish(at)
        project(at)
    block = min(256, rows_mine)
    scale = LOG2E / math.sqrt(HD)
    for lo in range(0, rows_mine, block):
        cols = pl.ds(pl.multiple_of(row_lo + lo, block), block)
        n = normed_t[:, cols].astype(F32).T.astype(BF)
        both = jnp.concatenate([n, n], axis=1)
        query[lo : lo + block, :] = (dot(both, w_pair[:, 0:width]) * scale).astype(BF)
        enc[lo : lo + block, :] = dot(n, w_enc[...]) + b_enc[...]

    q_step = min(256, rows_mine)
    k_step = 512
    ones = jnp.ones((k_step, HD), BF)

    @pl.loop(0, rows_mine // q_step)
    def _(number):
        lo = pl.multiple_of(number * q_step, q_step)
        q_rows = pl.ds(lo, q_step)
        cols = pl.ds(pl.multiple_of(row_lo + lo, q_step), q_step)
        table = jnp.concatenate(
            [mem_t[:, cols].astype(F32), jnp.zeros((HD - SLOTS, q_step), F32)], axis=0
        ).T.astype(BF)
        for head in range(HEADS):
            lanes = slice(head * HD, (head + 1) * HD)
            q = jnp.concatenate([query[q_rows, lanes], table], axis=1)
            peak = jnp.full((q_step, HD), -3e38, F32)
            for at in range(0, rows, k_step):
                k_rows = slice(at, at + k_step)
                k = jnp.concatenate([keys[k_rows, lanes], key_aug[k_rows, :]], axis=1)
                s = dot_nt(q, k)
                sbuf[head % 2, :, k_rows] = s
                for lo in range(0, k_step, HD):
                    peak = jnp.maximum(peak, s[:, lo : lo + HD])
            top = jnp.broadcast_to(jnp.max(peak, axis=1, keepdims=True), (q_step, HD))
            total = jnp.zeros((q_step, 2 * HD), F32)
            for at in range(0, rows, k_step):
                k_rows = slice(at, at + k_step)
                p = jnp.exp2(sbuf[head % 2, :, k_rows] - tile_lanes(top, k_step)).astype(BF)
                v = jnp.concatenate([vals[k_rows, lanes], ones], axis=1)
                total = total + dot(p, v)
            norm = total[:, HD:]
            att[q_rows, lanes] = total[:, :HD] / norm
            query_aug[head, q_rows, :] = aug_lanes(table, -(top + jnp.log2(norm)))

    wait_all(loads[3 * wide_blocks :])
    small[...] = jnp.zeros(small.shape, F32)

    def add_small(slot, value, wide):
        small[slot : slot + 1, 0:wide] += jnp.sum(value, axis=0, keepdims=True)

    def mean_of(v):
        return jnp.mean(v, axis=1, keepdims=True)

    for lo in range(0, rows_mine, block):
        at = slice(lo, lo + block)
        attended = att[at, :]
        attl = attended.astype(BF)
        fill(attl_s, at, attl)
        resid = enc[at, :] + dot(attl, w_out[...]) + b_out[...]
        ctr = resid - mean_of(resid)
        rstd1 = lax.rsqrt(mean_of(ctr * ctr) + EPS)
        n1 = ctr * rstd1
        o1 = n1 * gain_one[...] + shift_one[...]
        o1l = o1.astype(BF)
        fill(o1_s, at, o1l)
        pre = dot(o1l, w_up[...]) + b_up[...]
        cdf = 0.5 + 0.5 * lax.erf(pre * (1.0 / math.sqrt(2.0)))
        slope = cdf + pre * (jnp.exp(-0.5 * pre * pre) * (1.0 / math.sqrt(2.0 * math.pi)))
        actl = (pre * cdf).astype(BF)
        fill(act_s, at, actl)
        r2 = o1 + dot(actl, w_down[...]) + b_down[...]
        ctr2 = r2 - mean_of(r2)
        rstd2 = lax.rsqrt(mean_of(ctr2 * ctr2) + EPS)
        n2 = ctr2 * rstd2
        go = cot[at, :].astype(F32)
        cot[at, :] = (n2 * gain_two[...] + shift_two[...]).astype(BF)
        add_small(0, go * n2, width)
        add_small(1, go, width)
        dn = go * gain_two[...]
        g2 = rstd2 * (dn - mean_of(dn) - n2 * mean_of(dn * n2))
        gfl = g2.astype(BF)
        fill(gffn_s, at, gfl)
        add_small(2, g2, width)
        gpl = (dot_nt(gfl, w_down[...]) * slope).astype(BF)
        fill(gpre_s, at, gpl)
        add_small(3, gpl.astype(F32), hidden)
        g1 = dot_nt(gpl, w_up[...]) + g2
        add_small(4, g1 * n1, width)
        add_small(5, g1, width)
        dn1 = g1 * gain_one[...]
        gr = rstd1 * (dn1 - mean_of(dn1) - n1 * mean_of(dn1 * n1))
        add_small(6, gr, width)
        gbl = gr.astype(BF)
        fill(gbl_s, at, gbl)
        ga = dot_nt(gbl, w_out[...]).astype(BF)
        grad_att[at, :] = ga
        prod = ga.astype(F32) * attended
        zero = jnp.zeros((block, HD), BF)
        for head in range(HEADS):
            lanes = slice(head * HD, (head + 1) * HD)
            row_sum = jnp.sum(prod[:, lanes], axis=1, keepdims=True)
            att_aug[head, at, :] = aug_lanes(zero, jnp.broadcast_to(-row_sum, (block, HD)))

    store_out = pltpu.make_async_copy(cot, out_h, local_sem.at[3 * wide_blocks + 4])
    store_out.start()

    def pack(at, value):
        count = value.shape[0]
        early_x[at : at + count, :] = value[:, :half].astype(BF)
        early_x[early_size + at : early_size + at + count, :] = value[:, half:].astype(BF)

    own = pl.ds(row_lo, rows_mine)
    for i, part in enumerate(attl_s):
        pack(i * half, dot_tn(part[...], read(gbl_s)))
    base = width
    for i, part in enumerate(o1_s):
        up = dot_tn(part[...], read(gpre_s))
        for j in range(hidden // width):
            pack(base + j * width + i * half, up[:, j * width : (j + 1) * width])
    base = base + hidden
    for i, part in enumerate(act_s):
        pack(base + i * half, dot_tn(part[...], read(gffn_s)))
    base = base + hidden
    pack(base, dot(normed_t[:, own], read(gbl_s)))
    base = base + columns
    pack(base, jnp.concatenate([small[:, :width], small[:, width:]], axis=0))
    base = base + 16
    if base < early_size:
        pack(base, jnp.zeros((early_size - base, width), F32))
    early.stage(0)

    wide = HEADS // PASSES * HD
    grad_normed = sbuf.at[0, 0:columns, :]
    moment = sbuf.at[0, columns : 2 * columns, 0 : 3 * wide]
    mine = sbuf.at[1, 0:cols_mine, :]
    grad_own = sbuf.at[1, cols_mine : cols_mine + columns, 0:rows_mine]
    w_low = w_pair.at[0:columns, :]
    grad_own[...] = dot_nt(w_enc[...], read(gbl_s))
    chunks = rows // k_step
    plan = {}

    def place(when, stage):
        plan.setdefault(min(when, chunks * PASSES), []).append(stage)

    for number in range(1, early.stages):
        when = EARLY_AT[number - 1] if number <= len(EARLY_AT) else 16
        place(when * chunks * PASSES // 16, functools.partial(early.stage, number))
    for turn in range(PASSES - 1):
        for number in range(1, lates[turn].stages):
            when = LATE_AT[number - 1] if number <= len(LATE_AT) else 16
            place((turn + 1) * chunks + when * chunks // 8,
                  functools.partial(lates[turn].stage, number))

    order = bits_below(feat_count)
    index = {}
    for bit in order:
        for i in range(feat_count // (2 * bit)):
            index[bit, i] = len(index)

    def piece_at(number):
        return pl.ds(pl.multiple_of(number * k_step, k_step), k_step)

    def copy(bit, i, number):
        j = 1 - bit_of(me, bit) + 2 * i
        src = grad_low if bit == 1 else held
        at = j if bit == 1 else index[bit // 2, 0] + j
        return send(
            src.at[at, :, piece_at(number)], grad_in.at[index[bit, i], :, piece_at(number)],
            (rsend, rrecv), index[bit, i] * chunks + number, {"feat": flip(me, bit)},
        )

    def sum_start(level, number):
        bit = order[level]
        start_all([copy(bit, i, number) for i in range(feat_count // (2 * bit))])

    def sum_step(level, number):
        bit = order[level]
        cut = piece_at(number)
        for i in range(feat_count // (2 * bit)):
            copy(bit, i, number).wait()
            j = bit_of(me, bit) + 2 * i
            here = grad_low[j, :, cut] if bit == 1 else held[index[bit // 2, 0] + j, :, cut]
            total = here.astype(F32) + grad_in[index[bit, i], :, cut].astype(F32)
            if level + 1 < len(order):
                held[index[bit, i], :, cut] = total.astype(BF)
            else:
                mine[:, cut] = total
        if level + 1 < len(order):
            sum_start(level + 1, number)

    for turn in range(PASSES):
        heads = range(turn * HEADS // PASSES, (turn + 1) * HEADS // PASSES)
        at_pass = slice(turn * wide, (turn + 1) * wide)
        dq = att.at[:, at_pass]
        dq[...] = jnp.zeros((rows_mine, wide), F32)
        moment[...] = jnp.zeros(moment.shape, F32)
        w_kv = jnp.concatenate(
            [w_low[:, part * width + turn * wide : part * width + (turn + 1) * wide]
             for part in (1, 2)],
            axis=1,
        )

        @pl.loop(0, chunks)
        def _(number, turn=turn, heads=heads, dq=dq, w_kv=w_kv):
            k_rows = piece_at(number)
            aug = key_aug[k_rows, :]
            dks, dvs = [], []
            for head in heads:
                lanes = slice(head * HD, (head + 1) * HD)
                q = query[:, lanes]
                k = keys[k_rows, lanes]
                do = grad_att[:, lanes]
                s = dot_nt(
                    jnp.concatenate([k, aug], axis=1),
                    jnp.concatenate([q, query_aug[head]], axis=1),
                )
                p = jnp.exp2(s)
                dp = dot_nt(
                    jnp.concatenate([vals[k_rows, lanes], aug], axis=1),
                    jnp.concatenate([do, att_aug[head]], axis=1),
                )
                ds = (p * dp).astype(BF)
                dvs.append(dot(p.astype(BF), do).astype(BF))
                dks.append((dot(ds, q) * (1.0 / LOG2E)).astype(BF))
                into = slice((head - heads[0]) * HD, (head - heads[0] + 1) * HD)
                dq[:, into] += dot_tn(ds, k)
            grads = jnp.concatenate(dks + dvs, axis=1)
            moment[:, wide:] += dot(normed_t[:, k_rows], grads)
            product = dot_nt(w_kv, grads)
            if turn > 0:
                product = product + grad_normed[:, k_rows]
            if turn + 1 < PASSES:
                grad_normed[:, k_rows] = product
            else:
                for i in range(feat_count):
                    grad_low[i, :, k_rows] = product[i * cols_mine : (i + 1) * cols_mine, :].astype(
                        BF
                    )
                sum_start(0, number)

                @pl.when(number > 0)
                def _():
                    sum_step(0, number - 1)

            for when, stages in plan.items():
                if turn * chunks <= when < (turn + 1) * chunks:

                    @pl.when(number == when - turn * chunks)
                    def _(stages=stages):
                        for stage in stages:
                            stage()

        dql = (dq[...] * (1.0 / math.sqrt(HD))).astype(BF)
        moment[:, 0:wide] = dot(normed_t[:, own], dql)
        parts = jnp.concatenate(
            [moment[:, part * wide : (part + 1) * wide].astype(BF) for part in range(3)], axis=0
        )
        both = parts.shape[0] // 2
        for side in range(2):
            at = late_x[turn] + side * late_size
            stash[at : at + both, :] = parts[side * both : (side + 1) * both, :]
            if both < late_size:
                stash[at + both : at + late_size, :] = jnp.zeros((late_size - both, half), BF)
        lates[turn].stage(0)
        grad_own[...] += dot_nt(w_low[:, at_pass], dql)

    for i in range(feat_count):
        own_low[i] = grad_own[i * cols_mine : (i + 1) * cols_mine, :].astype(BF)
    swaps = []
    for number, other in enumerate(feat_others(me, feat_count)):
        swaps.append(
            send(own_low.at[other], own_in.at[me], (osend, orecv), number, {"feat": other})
        )
    start_all(swaps)
    own_in[me] = own_low[me]
    left = plan.get(chunks * PASSES, [])
    late = lates[-1]
    late.stage(1)
    sum_step(0, chunks - 1)
    for stage in left[:1]:
        stage()
    for level in range(1, len(order)):
        for number in range(chunks):
            sum_step(level, number)
    late.stage(2)
    wait_all(swaps)
    for i in range(feat_count):
        span = slice(i * rows_mine, (i + 1) * rows_mine)
        mine[:, span] += own_in[i].astype(F32)

    def gather(v, member):
        high, mid, small = split3(v)
        return dot_nt(high, member) + dot_nt(mid, member) + dot_nt(small, member)

    d_factor = jnp.zeros((cols_mine, SLOTS), F32)
    for cut in pieces:
        d_factor = d_factor + gather(mine[:, cut] * cent[:, cut], mem_t[:, cut])
    side = jnp.where(var > 0.25, 1.0, jnp.where(var == 0.25, 0.5, 0.0))
    d_var = d_factor * (-0.5) * factor / jnp.maximum(var, 0.25) * side
    pull = 2.0 * d_var / count
    d_mean = jnp.zeros((cols_mine, SLOTS), F32)
    for cut in pieces:
        dc = mine[:, cut] * dot_split(factor, mem_t[:, cut]) + cent[:, cut] * dot_split(
            pull, tr_t[:, cut]
        )
        grad_x[:, cut] = dc
        d_mean = d_mean - gather(dc, mem_t[:, cut])
    d_mean = d_mean / count
    for cut in pieces:
        grad_x[:, cut] = grad_x[:, cut] + dot_split(d_mean, tr_t[:, cut])
    for number in range(3, late.stages - 1):
        late.stage(number)
    for stage in left[1:]:
        stage()
    stores = [
        pltpu.make_async_copy(
            stash.at[pl.ds(at, count)], into, local_sem.at[3 * wide_blocks + 5 + i]
        )
        for i, (at, count, into) in enumerate(
            [(0, 2 * early_size, early_h)]
            + [
                (late_o[turn], 2 * late_size, late_h.at[pl.ds(turn * 2 * late_size, 2 * late_size)])
                for turn in range(PASSES)
            ]
        )
    ]
    start_all(stores[:-1])
    late.stage(late.stages - 1)
    stores[-1].start()
    store_out.wait()
    wait_all(stores)


def finish_kernel(
    early_h, late, w_enc, w_qkv_h, b_enc, out_in, grad_x_in,
    out, grad_x, g_w_enc, g_b_enc, g_w_qkv_h, g_b_query, g_b_value, g_w_out_h, g_b_out,
    g_gain_one, g_shift_one, g_w_up_h, g_b_up, g_w_down_h, g_b_down, g_gain_two, g_shift_two,
    early, w_qkv, g_w_qkv, g_w_out, g_w_up, g_w_down, moment_s, out_s, grad_x_s, sem,
):
    columns, width = w_enc.shape
    hidden = g_w_up.shape[1]
    cols_mine = g_w_enc.shape[0]
    places = [0]

    def copy(src, dst):
        places[0] += 1
        made = pltpu.make_async_copy(src, dst, sem.at[places[0] - 1])
        made.start()
        return made

    rest = width + 2 * hidden
    size = early.shape[0] // 2
    cuts = [
        pl.ds(rest, size - rest), pl.ds(0, width), pl.ds(width, hidden),
        pl.ds(width + hidden, hidden),
    ]
    loads = [
        [
            copy(
                early_h.at[pl.ds(side * size + cut.start, cut.size)],
                early.at[pl.ds(side * size + cut.start, cut.size)],
            )
            for side in range(2)
        ]
        for cut in cuts
    ]
    load_w = copy(w_qkv_h, w_qkv)
    passing = [copy(out_in, out_s), copy(grad_x_in, grad_x_s)]
    pending = []

    late_size = late.shape[0] // (2 * PASSES)
    wide = width // PASSES
    for turn in range(PASSES):
        starts = [(2 * turn + side) * late_size for side in range(2)]
        rows = jnp.concatenate([late[at : at + 3 * columns // 2, :] for at in starts], axis=0)
        for part in range(3):
            lo = part * width + turn * wide
            moment_s[:, lo : lo + wide] = rows[part * columns : (part + 1) * columns, :]
    bias = split3(b_enc[...])
    for lo in range(0, 3 * width, width):
        cut = slice(lo, lo + width)
        sums = moment_s[columns - 1 : columns, cut]
        outer = dot_tn(bias[0], sums) + dot_tn(bias[1], sums) + dot_tn(bias[2], sums)
        g_w_qkv[:, cut] = dot_tn(w_enc[...], moment_s[:, cut]) + outer
        lanes = pl.ds(lo, width)
        pending.append(copy(g_w_qkv.at[:, lanes], g_w_qkv_h.at[:, lanes]))

    wait_all(passing)
    pending += [copy(out_s, out), copy(grad_x_s, grad_x)]

    def take(lo, count):
        return jnp.concatenate(
            [early[lo : lo + count, :], early[size + lo : size + lo + count, :]], axis=1
        )

    step = 256
    wait_all(loads[1])
    for lo in range(0, width, step):
        g_w_out[lo : lo + step, :] = take(lo, step).astype(F32)
    pending.append(copy(g_w_out, g_w_out_h))
    wait_all(loads[2])
    for part in range(hidden // width):
        for lo in range(0, width, step):
            g_w_up[lo : lo + step, part * width : (part + 1) * width] = take(
                width + part * width + lo, step
            ).astype(F32)
    pending.append(copy(g_w_up, g_w_up_h))
    wait_all(loads[3])
    for lo in range(0, hidden, step):
        g_w_down[lo : lo + step, :] = take(width + hidden + lo, step).astype(F32)
    pending.append(copy(g_w_down, g_w_down_h))

    wait_all(loads[0])
    load_w.wait()
    first = pl.multiple_of(lax.axis_index("feat") * cols_mine, cols_mine)
    local = jnp.concatenate(
        [early[pl.ds(side * size + rest + first, cols_mine), :] for side in range(2)], axis=1
    )
    total = dot_nt(moment_s[pl.ds(first, cols_mine), :], w_qkv[...]) + local.astype(F32)
    column = lax.broadcasted_iota(jnp.int32, (cols_mine, 1), 0) + first
    g_w_enc[...] = jnp.where(column == columns - 1, 0.0, total)
    small = take(rest + columns, 16).astype(F32)
    last = moment_s[columns - 16 : columns, :]
    g_b_enc[...] = dot_nt(last, w_qkv[...])[15:16, :] + small[6:7, :]
    sums = last.astype(F32)[15:16, :]
    g_b_query[...] = sums[:, :width]
    g_b_value[...] = sums[:, 2 * width :]
    g_b_out[...] = small[6:7, :]
    g_gain_one[...] = small[4:5, :]
    g_shift_one[...] = small[5:6, :]
    g_b_up[...] = jnp.concatenate([small[3:4, :], small[11:12, :]], axis=1)
    g_b_down[...] = small[2:3, :]
    g_gain_two[...] = small[0:1, :]
    g_shift_two[...] = small[1:2, :]
    wait_all(pending)


def spec(kind):
    return pl.BlockSpec(memory_space={"v": pltpu.VMEM, "s": pltpu.SMEM, "h": pl.ANY}[kind])


def call(kernel, ins, args, outs, scratch, **params):
    return pl.pallas_call(
        kernel,
        out_shape=tuple(jax.ShapeDtypeStruct(shape, kind) for _, shape, kind in outs),
        in_specs=[spec(k) for k in ins],
        out_specs=tuple(spec(k) for k, _, _ in outs),
        scratch_shapes=[
            pltpu.SemaphoreType.DMA((entry,)) if isinstance(entry, int) else pltpu.VMEM(*entry)
            for entry in scratch
        ],
        compiler_params=pltpu.CompilerParams(vmem_limit_bytes=VMEM_BYTES, **params),
    )(*args)


def per_device(
    features, lengths, train_counts, used_features, w_enc, b_enc, w_qkv, b_query, b_value,
    w_out, b_out, gain_one, shift_one, w_up, b_up, w_down, b_down, gain_two, shift_two, cotangent,
):
    places = {"feat": lax.axis_size("feat"), "rows": lax.axis_size("rows")}
    feat_count = places["feat"]
    rows, cols_mine = features.shape
    columns = cols_mine * feat_count
    width = w_qkv.shape[0]
    hidden = w_up.shape[1]
    rows_mine = rows // feat_count
    half = width // 2
    early_group, late_group = 2, 4
    early_rows, early_parts, early_sems, early_land = reduce_plan(
        width + 2 * hidden + columns + 16, places, early_group
    )
    late_rows, late_parts, late_sems, late_land = reduce_plan(
        3 * columns // 2, places, late_group
    )
    stash_rows = max(
        rows_mine * (4 * width + 2 * hidden) // half, 2 * early_rows + 4 * PASSES * late_rows
    )
    row = lambda v: v.reshape(1, -1)
    gather_sems = 5 * (feat_count - 1)
    out, early, late, grad_x, w_enc_all = call(
        functools.partial(
            layer_kernel, places=places, early_parts=early_parts, early_group=early_group,
            late_parts=late_parts, late_group=late_group,
        ),
        "sss" + "v" * 12 + "h" * 5,
        (
            lengths, train_counts, used_features, features.T, w_enc, row(b_enc), row(b_query),
            row(b_value), row(b_out), row(gain_one), row(shift_one), row(b_up), row(b_down),
            row(gain_two), row(shift_two), w_qkv, w_out, w_up, w_down, cotangent,
        ),
        [
            ("h", (rows_mine, width), BF), ("h", (2 * early_rows, half), BF),
            ("h", (PASSES * 2 * late_rows, half), BF), ("v", (cols_mine, rows), F32),
            ("v", (columns, width), BF),
        ],
        [
            (w_out.shape, BF), (w_up.shape, BF), (w_down.shape, BF),
            ((rows_mine, width), BF),
            ((SLOTS, rows), BF), ((SLOTS, rows), BF), ((8, SLOTS), F32), ((rows, HD), BF),
            ((cols_mine, rows), F32), ((columns, rows), BF), ((2 * columns, 3 * width), BF),
            ((rows, width), BF), ((rows, width), BF), ((rows_mine, width), BF),
            ((rows_mine, width), F32), ((rows_mine, width), F32),
            ((HEADS, rows_mine, HD), BF), ((rows_mine, width), BF), ((HEADS, rows_mine, HD), BF),
            ((2, min(256, rows_mine), rows), F32),
            ((8, hidden), F32), ((stash_rows, half), BF), ((2 * early_rows, half), BF),
            ((early_rows, half), BF), ((early_land, half), BF),
            ((feat_count, cols_mine, rows), BF),
            ((PASSES, late_rows, half), BF), ((PASSES, late_land, half), BF),
            ((feat_count // 2, cols_mine, rows), BF), ((feat_count - 1, cols_mine, rows), BF),
            ((feat_count, cols_mine, rows_mine), BF), ((feat_count, cols_mine, rows_mine), BF),
            3 * (width // half) + 5 + 1 + PASSES, gather_sems, gather_sems, early_sems, early_sems,
            PASSES * late_sems, PASSES * late_sems,
            (feat_count - 1) * (rows // 512), (feat_count - 1) * (rows // 512), feat_count - 1,
            feat_count - 1,
        ],
        collective_id=0, has_side_effects=True,
    )
    vector = ("v", (1, width), F32)
    grads = call(
        finish_kernel,
        "hvvhvhh",
        (early, late, w_enc_all, w_qkv, row(b_enc), out, grad_x),
        [
            ("h", (rows_mine, width), BF), ("h", (cols_mine, rows), F32),
            ("v", (cols_mine, width), F32), vector,
            ("h", (width, 3 * width), F32), vector, vector, ("h", (width, width), F32), vector,
            vector, vector, ("h", (width, hidden), F32), ("v", (1, hidden), F32),
            ("h", (hidden, width), F32), vector, vector, vector,
        ],
        [
            ((2 * early_rows, half), BF), (w_qkv.shape, BF), ((width, 3 * width), F32),
            ((width, width), F32), ((width, hidden), F32), ((hidden, width), F32),
            ((columns, 3 * width), BF), ((rows_mine, width), BF), ((cols_mine, rows), F32), 20,
        ],
    )
    grads = [g.reshape(-1) if g.shape[0] == 1 else g for g in grads]
    return (grads[0], grads[1].T) + tuple(grads[2:])


def solution(mesh):
    whole = P()
    in_specs = (
        (P("rows", "feat"),) + (P("rows", None),) * 3 + (P("feat", None),) + (whole,) * 14
        + (P(("rows", "feat"), None),)
    )
    out_specs = (
        (P(("rows", "feat"), None), P("rows", "feat"), P("feat", None)) + (whole,) * 14
    )
    return jax.shard_map(
        per_device, mesh=mesh, in_specs=in_specs, out_specs=out_specs, check_vma=False
    )
```

time: 151 us -> 140 us (0.927)
  Pallas kernels: 147 us -> 139 us
  local copies, waits for them, and re-layouts: 3.12 us -> 0 us
    pallas_call x2, Pallas kernels: 147 us -> 139 us  [call(): pl.pallas_call(kernel, out_shape=tuple((jax.ShapeDtypeStruct(shape, kind)...]
    unnamed x4 -> x0, local copies, waits for them, and re-layouts: 3.12 us -> none
where the time goes in v3:
time: 140 us
  Pallas kernels  139 us (99%)
    pallas_call x2, Pallas kernels, call(): pl.pallas_call(kernel, out_shape=tuple((jax.ShapeDtypeStruct(shape, kind)...  139 us

profile of v3, /device:TPU:0, one launch (start us, length us, event | category | flops | bytes accessed | tf_op | source)
XLA Modules:
  0.0 140.2 jit_solution(15750215652279171746)
XLA Ops:
  0.7 130.6 %shard_map.323 = (bf16[1024,512]{1,0:T(8,128)(2,1)}, bf16[5632,256]{1,0:T(8,128)(2,1)}, bf16[1024,256]{1,0:T(8,128)(2,1)}, f32[32,4096]{1,0:T(8,128)}, bf16[128,512]{1,0:T(8,128)(2,1)}) custom-call(s32[1,6]{1,0:T(1,128)} %lengths.1, s32[1,6]{1,0:T(1,128)} %trains.1, s32[1,6]{1,0:T(1,128)} %used.1, bf16[32,4096]{1,0:T(8,128)(2,1)} %bitcast.22, ...), custom_call_target="tpu_custom_call" | custom-call | tf_op jit(solution)/shard_map/pallas_call | solution.py:939
  131.3 8.7 %shard_map.324 = (bf16[1024,512]{1,0:T(8,128)(2,1)}, f32[32,4096]{1,0:T(8,128)}, f32[32,512]{1,0:T(8,128)}, f32[1,512]{1,0:T(1,128)}, f32[512,1536]{1,0:T(8,128)...) custom-call(bf16[5632,256]{1,0:T(8,128)(2,1)} %get-tuple-element.39., ...), custom_call_target="tpu_custom_call" | custom-call | tf_op jit(solution)/shard_map/pallas_call | solution.py:939

commit v4 on v3

--- a/solution.py
+++ b/solution.py
@@ -451,10 +451,6 @@
     factor = jnp.where(
         column < tab[2:3, :], lax.rsqrt(jnp.maximum(var, 0.25)) * tab[1:2, :], 0.0
     )
-    for cut in pieces:
-        normed_t[pl.ds(col_lo, cols_mine), cut] = jnp.where(
-            is_last, 1.0, cent[:, cut] * dot_split(factor, mem_t[:, cut])
-        ).astype(BF)
     w_enc[pl.ds(col_lo, cols_mine), :] = w_mine[...]
     await_greetings(peers)
     steps = len(gather_steps(feat_count))
@@ -464,6 +460,10 @@
     piece = rows // splits
     gather_x = GatherFeat(normed_t, cols_mine, piece, (gsend, grecv), steps, feat_count)
     for at in range(splits):
+        for cut in pieces[at * piece // step : (at + 1) * piece // step]:
+            normed_t[pl.ds(col_lo, cols_mine), cut] = jnp.where(
+                is_last, 1.0, cent[:, cut] * dot_split(factor, mem_t[:, cut])
+            ).astype(BF)
         gather_x.start(at)
 
     key_masks((lengths, trains), key_aug)
@@ -785,8 +785,12 @@
         mine[:, span] += own_in[i].astype(F32)
 
     def gather(v, member):
-        high, mid, small = split3(v)
-        return dot_nt(high, member) + dot_nt(mid, member) + dot_nt(small, member)
+        high, mid, _ = split3(v)
+        return dot_nt(high, member) + dot_nt(mid, member)
+
+    def expand(v, member):
+        high, mid, _ = split3(v)
+        return dot(high, member) + dot(mid, member)
 
     d_factor = jnp.zeros((cols_mine, SLOTS), F32)
     for cut in pieces:
@@ -796,14 +800,14 @@
     pull = 2.0 * d_var / count
     d_mean = jnp.zeros((cols_mine, SLOTS), F32)
     for cut in pieces:
-        dc = mine[:, cut] * dot_split(factor, mem_t[:, cut]) + cent[:, cut] * dot_split(
+        dc = mine[:, cut] * expand(factor, mem_t[:, cut]) + cent[:, cut] * expand(
             pull, tr_t[:, cut]
         )
         grad_x[:, cut] = dc
         d_mean = d_mean - gather(dc, mem_t[:, cut])
     d_mean = d_mean / count
     for cut in pieces:
-        grad_x[:, cut] = grad_x[:, cut] + dot_split(d_mean, tr_t[:, cut])
+        grad_x[:, cut] = grad_x[:, cut] + expand(d_mean, tr_t[:, cut])
     for number in range(3, late.stages - 1):
         late.stage(number)
     for stage in left[1:]:

time: 140 us -> 140 us (level)
  no operation moved by 1% of the time
where the time goes in v4:
time: 140 us
  Pallas kernels  139 us (99%)
    pallas_call x2, Pallas kernels, call(): pl.pallas_call(kernel, out_shape=tuple((jax.ShapeDtypeStruct(shape, kind)...  139 us

profile of v4, /device:TPU:0, one launch (start us, length us, event | category | flops | bytes accessed | tf_op | source)
XLA Modules:
  0.0 140.2 jit_solution(63043351245100298)
XLA Ops:
  0.7 130.7 %shard_map.323 = (bf16[1024,512]{1,0:T(8,128)(2,1)}, bf16[5632,256]{1,0:T(8,128)(2,1)}, bf16[1024,256]{1,0:T(8,128)(2,1)}, f32[32,4096]{1,0:T(8,128)}, bf16[128,512]{1,0:T(8,128)(2,1)}) custom-call(s32[1,6]{1,0:T(1,128)} %lengths.1, s32[1,6]{1,0:T(1,128)} %trains.1, s32[1,6]{1,0:T(1,128)} %used.1, bf16[32,4096]{1,0:T(8,128)(2,1)} %bitcast.22, ...), custom_call_target="tpu_custom_call" | custom-call | tf_op jit(solution)/shard_map/pallas_call | solution.py:943
  131.3 8.7 %shard_map.324 = (bf16[1024,512]{1,0:T(8,128)(2,1)}, f32[32,4096]{1,0:T(8,128)}, f32[32,512]{1,0:T(8,128)}, f32[1,512]{1,0:T(1,128)}, f32[512,1536]{1,0:T(8,128)...) custom-call(bf16[5632,256]{1,0:T(8,128)(2,1)} %get-tuple-element.39., ...), custom_call_target="tpu_custom_call" | custom-call | tf_op jit(solution)/shard_map/pallas_call | solution.py:943
